TPU v7x, 128 devices: a whole 4x4x4 slice. The times are simulated.
128 devices in a mesh: seq: 64 (over y, z, x), head: 2 (over core).
Axes of the slice: x: 4, y: 4, z: 4, core: 2. Of those that a mesh axis runs over, the one named last changes fastest.
Arguments:
- query: bfloat16 [256, 4096], P('head'), may hold values from -16 to 16
- d_out: bfloat16 [256, 4096], P('head'), may hold values from -6144 to 6144
- out_fwd: bfloat16 [256, 4096], P('head'), may hold values from -6 to 6
- prompt_keys: bfloat16 [65536, 2048], P('seq', 'head'), may hold values from -16 to 16
- prompt_value_rows: bfloat16 [65536, 2048], P('seq', 'head'), may hold values from -6 to 6
- sibling_key_rows: bfloat16 [256, 2048], P('head'), may hold values from -5 to 5
- sibling_value_rows: bfloat16 [256, 2048], P('head'), may hold values from -6 to 6
- parents: int32 [8], replicated, may hold values from -1 to 6
Outputs:
- grad_query: bfloat16 [256, 4096], P('head')
- grad_prompt_keys: bfloat16 [65536, 2048], P('seq', 'head')
- grad_prompt_values: bfloat16 [65536, 2048], P('seq', 'head')
- grad_sib_keys: bfloat16 [256, 2048], P('head')
- grad_sib_values: bfloat16 [256, 2048], P('head')
All inputs are finite; a program needn't handle non-finite values.
Results may differ from a plain program's by a relative error of at most 0.0054.
Values may be sent and summed in bfloat16 or wider, within the bound.
No kernel may reach another device: no remote copies, remote signals or barrier semaphores. Data moves between devices by JAX's collectives and lax.ppermute only.
A program may use at most 128 MiB of HBM per device.

v0:
```python
import jax
import jax.numpy as jnp
from jax import lax
from jax.sharding import PartitionSpec as P

HEAD_DIMENSION = 128


score_scale = 144.0 ** (-0.5)


def ancestry(parents):
    count = parents.shape[0]
    identity = jnp.eye(count, dtype=jnp.float32)
    link_mat = (parents[:, None] == jnp.arange(count, dtype=jnp.int32)[None, :]).astype(jnp.float32)
    reached = identity
    for turn_idx in range(count):
        reached = jnp.minimum(
            1.0, identity + jnp.dot(link_mat, reached, precision=lax.Precision.HIGHEST)
        )
    return reached


def tree_mask(parents, step_len):
    reached = ancestry(parents) > 0.5
    total_tok = parents.shape[0] * step_len
    position = jnp.arange(total_tok, dtype=jnp.int32)
    step_of = position // step_len
    in_step = position % step_len
    same_step = step_of[:, None] == step_of[None, :]
    return reached[step_of[:, None], step_of[None, :]] & (
        jnp.logical_not(same_step) | (in_step[None, :] <= in_step[:, None])
    )


def local(
    query,
    d_out,
    out_fwd,
    prompt_keys,
    prompt_value_rows,
    sibling_key_rows,
    sibling_value_rows,
    parents,
):
    f32 = jnp.float32
    kv_heads = prompt_keys.shape[1] // HEAD_DIMENSION
    arrived = (
        lax.all_to_all(query, "head", split_axis=1, concat_axis=0, tiled=True),
        lax.all_to_all(d_out, "head", split_axis=1, concat_axis=0, tiled=True),
        lax.all_to_all(out_fwd, "head", split_axis=1, concat_axis=0, tiled=True),
        lax.all_to_all(sibling_key_rows, "head", split_axis=1, concat_axis=0, tiled=True),
        lax.all_to_all(sibling_value_rows, "head", split_axis=1, concat_axis=0, tiled=True),
    )
    q_local, do_local, o_local, ks_local, vs_local = arrived
    tokens = q_local.shape[0]
    heads_per_group = q_local.shape[1] // (kv_heads * HEAD_DIMENSION)
    do_heads = do_local.reshape(tokens, kv_heads, heads_per_group, HEAD_DIMENSION)
    o_heads = o_local.reshape(tokens, kv_heads, heads_per_group, HEAD_DIMENSION)
    out_dot = jnp.sum(do_heads.astype(f32) * o_heads.astype(f32), axis=-1).transpose(1, 0, 2)
    key_rows = prompt_keys.shape[0]
    allowed = tree_mask(parents, tokens // parents.shape[0])
    key_mask = allowed[None, :, None, :]
    q_heads = q_local.reshape(tokens, kv_heads, heads_per_group, HEAD_DIMENSION)
    kp_heads = prompt_keys.reshape(key_rows, kv_heads, HEAD_DIMENSION)
    vp_heads = prompt_value_rows.reshape(key_rows, kv_heads, HEAD_DIMENSION)
    ks_heads = ks_local.reshape(tokens, kv_heads, HEAD_DIMENSION)
    vs_heads = vs_local.reshape(tokens, kv_heads, HEAD_DIMENSION)
    prompt_scores = score_scale * jnp.einsum(
        "thgd,rhd->htgr", q_heads, kp_heads, preferred_element_type=f32
    )
    sib_scores = score_scale * jnp.einsum(
        "thgd,uhd->htgu", q_heads, ks_heads, preferred_element_type=f32
    )
    masked = jnp.where(key_mask, sib_scores, -jnp.inf)
    is_first = lax.axis_index("seq") == 0
    local_top = jnp.maximum(prompt_scores.max(-1), jnp.where(is_first, masked.max(-1), -jnp.inf))
    row_top = lax.pmax(local_top, "seq")
    prompt_part = jnp.exp(prompt_scores - row_top[..., None]).sum(-1)
    sib_part = jnp.exp(masked - row_top[..., None]).sum(-1)
    row_total = lax.psum(prompt_part + jnp.where(is_first, sib_part, 0.0), "seq")
    log_total = row_top + jnp.log(row_total)
    prompt_probs = jnp.exp(prompt_scores - log_total[..., None])
    sib_probs = jnp.exp(masked - log_total[..., None])
    prompt_dp = jnp.einsum("thgd,rhd->htgr", do_heads, vp_heads, preferred_element_type=f32)
    sib_dp = jnp.einsum("thgd,uhd->htgu", do_heads, vs_heads, preferred_element_type=f32)
    prompt_ds = (prompt_probs * (prompt_dp - out_dot[..., None])).astype(jnp.bfloat16)
    sib_ds = (sib_probs * (sib_dp - out_dot[..., None])).astype(jnp.bfloat16)
    prompt_pb = prompt_probs.astype(jnp.bfloat16)
    sib_pb = sib_probs.astype(jnp.bfloat16)
    grad_prompt = jnp.einsum("htgr,rhd->thgd", prompt_ds, kp_heads, preferred_element_type=f32)
    grad_sib = jnp.einsum("htgu,uhd->thgd", sib_ds, ks_heads, preferred_element_type=f32)
    query_terms = (grad_prompt + jnp.where(is_first, grad_sib, 0.0)).reshape(
        tokens, kv_heads * heads_per_group * HEAD_DIMENSION
    )
    grad_kp = (
        (score_scale * jnp.einsum("htgr,thgd->rhd", prompt_ds, q_heads, preferred_element_type=f32))
        .astype(jnp.bfloat16)
        .reshape(key_rows, kv_heads * HEAD_DIMENSION)
    )
    grad_vp = (
        jnp.einsum("htgr,thgd->rhd", prompt_pb, do_heads, preferred_element_type=f32)
        .astype(jnp.bfloat16)
        .reshape(key_rows, kv_heads * HEAD_DIMENSION)
    )
    grad_ks = (
        (score_scale * jnp.einsum("htgu,thgd->uhd", sib_ds, q_heads, preferred_element_type=f32))
        .astype(jnp.bfloat16)
        .reshape(tokens, kv_heads * HEAD_DIMENSION)
    )
    grad_vs = (
        jnp.einsum("htgu,thgd->uhd", sib_pb, do_heads, preferred_element_type=f32)
        .astype(jnp.bfloat16)
        .reshape(tokens, kv_heads * HEAD_DIMENSION)
    )
    grad_q = (score_scale * lax.psum(query_terms, "seq")).astype(jnp.bfloat16)
    returned = (
        lax.all_to_all(grad_q, "head", split_axis=0, concat_axis=1, tiled=True),
        lax.all_to_all(grad_ks, "head", split_axis=0, concat_axis=1, tiled=True),
        lax.all_to_all(grad_vs, "head", split_axis=0, concat_axis=1, tiled=True),
    )
    return (returned[0], grad_kp, grad_vp, returned[1], returned[2])


def solution(mesh):
    in_specs = (
        P("head", None),
        P("head", None),
        P("head", None),
        P("seq", "head"),
        P("seq", "head"),
        P("head", None),
        P("head", None),
        P(),
    )
    out_specs = (
        P("head", None),
        P("seq", "head"),
        P("seq", "head"),
        P("head", None),
        P("head", None),
    )
    return jax.shard_map(local, mesh=mesh, in_specs=in_specs, out_specs=out_specs, check_vma=False)
```

profile of v0, /device:TPU:1, one launch (start us, length us, event | category | flops | bytes accessed | tf_op | source)
XLA Modules:
  0.0 1473.1 jit_solution(4569511011312579589)
XLA Ops:
  7.2 1.9 copy.217
  9.0 4.9 all-to-all-start.1
  13.9 0.8 fusion.36
  14.8 0.8 fusion.35
  15.6 0.8 fusion.34
  16.5 0.8 fusion.33
  17.3 0.8 fusion.32
  18.2 0.8 fusion.31
  19.0 0.8 fusion.30
  19.9 0.9 fusion.37
  21.0 529.9 %gather_fusion = pred[65536]{0:T(1024)(128)(4,1)S(1)} fusion(pred[8,8]{1,0:T(8,128)(4,1)S(1)} %fusion.37, s32[65536]{0:T(1024)S(1)} %bitcast.114), kind=kCustom, calls=%fused_computation | custom fusion | bytes 655360 | tf_op jit(solution)/shard_map/gather | solution.py:31
  551.3 0.8 copy.216
  552.2 3.5 all-to-all-start.4
  555.8 1.1 copy.157
  556.9 1.0 copy.215
  558.0 3.6 all-to-all-start
  561.6 0.9 copy.183
  562.4 2.3 copy.214
  564.8 3.6 all-to-all-start.2
  568.3 1.5 reshape.197
  569.9 1.0 copy.213
  570.9 4.4 all-to-all-start.3
  575.6 0.8 reshape.200
  576.3 0.9 all-to-all-done.3
  577.2 1.5 convert_bitcast_fusion
  578.7 2.8 reshape.206
  581.5 3.9 multiply_reduce_fusion.1
  585.4 0.4 copy.126
  585.8 3.6 copy.179
  589.3 3.2 copy.153
  592.6 3.5 copy.182
  596.1 9.4 multiply_reduce_fusion
  605.6 2.9 fusion.7
  608.5 295.3 %pmax.7 = f32[8,256,2]{1,2,0:T(2,128)S(1)} all-reduce(f32[8,256,2]{1,2,0:T(2,128)S(1)} %select_maximum_fusion), channel_id=1, replica_groups=mesh['seq'=64,'head'=2] {'seq'}, use_global_device_ids=true, to_apply=%region_2.3 | all-reduce | flops 4096 | bytes 32768 | tf_op jit(solution)/shard_map/pmax | solution.py:78
  903.8 3.1 exponential_reduce_fusion.1
  906.9 7.7 exponential_reduce_fusion
  914.6 286.4 %psum.14 = f32[8,256,2]{1,2,0:T(2,128)S(1)} all-reduce(f32[8,256,2]{1,2,0:T(2,128)S(1)} %select_add_fusion.1), channel_id=1, replica_groups=mesh['seq'=64,'head'=2] {'seq'}, use_global_device_ids=true, to_apply=%region_5.6 | all-reduce | flops 4096 | bytes 32768 | tf_op jit(solution)/shard_map/psum | solution.py:81
  1201.0 5.0 multiply_convert_fusion.1
  1206.0 9.4 multiply_convert_fusion
  1215.5 2.9 fusion.63
  1218.4 0.8 copy-done
  1219.2 1.8 select_add_fusion
  1221.0 3.5 fusion.26
  1224.5 0.3 copy.143
  1224.9 1.0 all_to_all.122
  1225.9 114.4 %all-to-all-start.7 = ((bf16[2,128,1024]{2,1,0:T(8,128)(2,1)}), bf16[2,128,1024]{2,1,0:T(8,128)(2,1)S(1)}, u32[]{:S(2)}, u32[]{:S(2)}) async-start(bf16[2,128,1024]{2,1,0:T(8,128)(2,1)} %all_to_all.122), calls=%async_computation.7 | async-start | bytes 1048576 | tf_op jit(solution)/shard_map/all_to_all | solution.py:120
  1340.3 2.3 fusion.25
  1342.6 0.3 copy.140
  1343.0 1.0 all_to_all.118
  1344.0 3.7 all-to-all-start.6
  1347.7 1.0 copy.144
  1348.8 2.0 copy.149
  1350.8 0.3 copy.141
  1351.1 1.0 copy.148
  1352.1 6.4 fusion.5
  1358.5 3.9 copy.146
  1362.4 7.9 bitcast_convert_fusion
  1370.4 2.6 copy.147
  1372.9 81.9 %all-reduce.2.cloned.1.call-done = f32[256,2048]{0,1:T(8,128)} async-done(((f32[256,2048]{0,1:T(8,128)}), f32[256,2048]{0,1:T(8,128)}) %all-reduce.2.cloned.1.call-update) | async-done | bytes 2097168 | tf_op jit(solution)/shard_map/psum | solution.py:116
  1454.9 1.8 multiply_convert_fusion.2
  1456.7 0.6 copy.135
  1457.3 7.0 all_to_all.134
  1464.3 0.7 copy.136
  1465.0 1.3 copy.145
  (36 shorter events, 1.0 us)
Async XLA Ops:
  9.0 543.1 %all-to-all-start.1 = ((bf16[128,2,1024]{2,0,1:T(8,128)(2,1)}), bf16[128,2,1024]{2,0,1:T(8,128)(2,1)S(1)}, u32[]{:S(2)}, u32[]{:S(2)}) async-start(bf16[128,2,1024]{2,0,1:T(8,128)(2,1)} %bitcast.110), calls=%async_computation.1 | async-start | bytes 1048576 | tf_op jit(solution)/shard_map/all_to_all | solution.py:52
  21.0 530.3 %copy-start.8 = (bf16[128,2048]{1,0:T(8,128)(2,1)S(1)}, bf16[128,2048]{1,0:T(8,128)(2,1)}, u32[]{:S(2)}) copy-start(bf16[128,2048]{1,0:T(8,128)(2,1)} %param.14) | copy-start | bytes 1572868
  550.9 6.0 copy-start.6
  552.2 5.8 all-to-all-start.4
  558.0 6.8 all-to-all-start
  561.5 8.3 copy-start.7
  564.8 6.2 all-to-all-start.2
  570.9 6.3 all-to-all-start.3
  575.4 879.5 %all-reduce.2.cloned.1.call-start = ((), (), s32[]{:S(2)}) async-start(), calls=%async_computation.8 | async-start | bytes 4194304 | tf_op jit(solution)/shard_map/psum | solution.py:116
  596.1 9.4 copy-start.1
  596.1 9.4 copy-start.3
  1215.5 3.7 copy-start
  1215.5 3.7 copy-start.4
  1215.5 3.7 copy-start.5
  1221.0 119.3 %copy-start.2 = (bf16[256,8,2,128]{3,2,1,0:T(2,128)(2,1)S(1)}, bf16[256,8,2,128]{3,2,1,0:T(2,128)(2,1)}, u32[]{:S(2)}) copy-start(bf16[256,8,2,128]{3,2,1,0:T(2,128)(2,1)} %reshape.197) | copy-start | bytes 3145732
  1225.9 118.1 %all-to-all-start.7 = ((bf16[2,128,1024]{2,1,0:T(8,128)(2,1)}), bf16[2,128,1024]{2,1,0:T(8,128)(2,1)S(1)}, u32[]{:S(2)}, u32[]{:S(2)}) async-start(bf16[2,128,1024]{2,1,0:T(8,128)(2,1)} %all_to_all.122), calls=%async_computation.7 | async-start | bytes 1048576 | tf_op jit(solution)/shard_map/all_to_all | solution.py:120
  1344.0 6.8 all-to-all-start.6
Sparse Core Ops, SparseCore 0:
  1221.1 233.6 all-reduce.1
where the time goes:
time: 1470 us
  blocking collectives  589 us (40%)
  local copies, waits for them, and re-layouts  572 us (39%)
  starting transfers between devices  138 us (9%)
  waiting for transfers between devices  82.9 us (6%)
  matrix products  58.4 us (4%)
  other arithmetic  18.2 us (1%)
    gather x2, local copies, waits for them, and re-layouts, tree_mask(): reached[step_of[:, None], step_of[None, :]]  530 us
    pmax x1, blocking collectives, local(): row_top = lax.pmax(local_top, 'seq')  295 us
    psum x1, blocking collectives, local(): lax.psum(prompt_part + jnp.where(is_first, sib_part, 0.0), 'seq')  286 us
    all_to_all x1, starting transfers between devices, local(): lax.all_to_all(grad_vs, 'head', split_axis=0, concat_axis=1, tiled=True)  114 us
    psum x1, waiting for transfers between devices, local(): grad_q = (score_scale * lax.psum(query_terms, 'seq')).astype(jnp.bfloat16)  81.9 us
  transfers between devices with their start and end apart: 8, of which 2 were waited for; matrix products, arithmetic and copies ran while one was open for 39% of the time, Pallas kernels for 0%

commit v1 on v0

v1 whole, which is shorter than its diff:
```python
import functools
import math

import jax
import jax.numpy as jnp
from jax import lax
from jax.experimental import pallas as pl
from jax.experimental.pallas import tpu as pltpu
from jax.sharding import PartitionSpec as P

f32 = jnp.float32
bf16 = jnp.bfloat16

D = 128
GROUP = 2
STEP_LEN = 32
SCALE = 144.0 ** (-0.5)
SCALE2 = SCALE * math.log2(math.e)
MASKED = -1e30
TOTAL_LOW, TOTAL_HIGH = 2.0**-60, 2.0**60
SWAP = [(0, 1), (1, 0)]
RADIX = 4
PAIR = 2
VMEM_LIMIT = 20 * 1024 * 1024

CHUNK = 2 * STEP_LEN
STAT_ROWS = 16


def dot_nt(a, b):
    return lax.dot_general(a, b, (((1,), (1,)), ((), ())), preferred_element_type=f32)


def dot_tn(a, b):
    return lax.dot_general(a, b, (((0,), (0,)), ((), ())), preferred_element_type=f32)


def dot_nn(a, b):
    return jnp.dot(a, b, preferred_element_type=f32)


def fold8(x, op):
    return op(x.reshape(x.shape[0] // 8, 8, x.shape[1]), axis=0)


def head_columns(head, width):
    return pl.ds(pl.multiple_of(head * width, width), width)


def head_rows(own, other, head):
    at = head_columns(head, GROUP * D)
    mine, theirs = own[:, at], other[:, at]
    return jnp.concatenate([x[:, g * D : (g + 1) * D] for g in range(GROUP) for x in (mine, theirs)], axis=0)


def out_dot_kernel(do, o, out):
    ones = jnp.ones((8, D), bf16)
    for head in range(out.shape[0]):
        at = slice(head * D, (head + 1) * D)
        product = do[:, at].astype(f32) * o[:, at].astype(f32)
        high = product.astype(bf16)
        low = (product - high.astype(f32)).astype(bf16)
        out[head : head + 1, :] = (dot_nt(ones, high) + dot_nt(ones, low))[0:1]


def finish_head(keys, probs, dprobs, out_dot, reference, probs_ref, ds_ref, pay_ref, stat_ref, head, k0):
    rows = probs.shape[1]
    probs_ref[head] = probs.astype(bf16)
    dscores = (probs * (dprobs - out_dot)).astype(bf16)
    ds_ref[head] = dscores
    total = jnp.sum(fold8(probs, jnp.sum), axis=0, keepdims=True)
    grad = dot_tn(keys, dscores).T.astype(bf16)
    stat_ref[0, pl.ds(head, 1), :] = reference
    stat_ref[1, pl.ds(head, 1), :] = total
    high = total.astype(bf16).astype(f32)
    stats = [reference, high, total - high]
    for g in range(GROUP):
        own, other = g * 2 * D, (g * 2 + 1) * D
        parts = [x[:, at : at + D] for at in (own, other) for x in stats]
        block = jnp.concatenate(parts + [jnp.zeros((STAT_ROWS - len(parts), D), f32)], axis=0).astype(bf16)
        for blk in range(D // STEP_LEN):
            k, at = k0 + g * (D // STEP_LEN) + blk, blk * STEP_LEN
            pay_ref[k, 0:STEP_LEN, :] = grad[own + at : own + at + STEP_LEN]
            pay_ref[k, STEP_LEN:CHUNK, :] = grad[other + at : other + at + STEP_LEN]
            pay_ref[k, CHUNK:, :] = block
    return total


def attend(keys, values, q_rows, do_rows, out_dot, mask, probs_ref, ds_ref, pay_ref, stat_ref, head, k0):
    rows = q_rows.shape[0]

    def masked(scores):
        return scores if mask is None else jnp.where(mask, scores, MASKED)

    def run(reference):
        scores = masked(dot_nt(keys, q_rows)) * SCALE2
        probs = jnp.exp2(scores if reference is None else scores - reference)
        held = jnp.zeros((1, rows), f32) if reference is None else reference
        return finish_head(
            keys, probs, dot_nt(values, do_rows), out_dot, held, probs_ref, ds_ref, pay_ref, stat_ref, head, k0
        )

    total = run(None)
    in_range = (jnp.min(total) > TOTAL_LOW) & (jnp.max(total) < TOTAL_HIGH)

    @pl.when(jnp.logical_not(in_range))
    def _():
        top = jnp.max(fold8(masked(dot_nt(keys, q_rows)), jnp.max), axis=0, keepdims=True)
        run((top * SCALE2).astype(bf16).astype(f32))


def row_dots(own, other, head):
    parts = [x[pl.ds(GROUP * head + g, 1), :] for g in range(GROUP) for x in (own, other)]
    return jnp.concatenate(parts, axis=1)


def prompt_kernel(place, q, qx, do, dox, dots, dotsx, kp, vp, probs, ds, pay, stat):
    kv = probs.shape[0]
    for i in range(PAIR):
        head = pl.program_id(0) * PAIR + i
        wide = place[1] * kv + head
        attend(
            kp[:, head_columns(head, D)],
            vp[:, head_columns(head, D)],
            head_rows(q, qx, wide),
            head_rows(do, dox, wide),
            row_dots(dots, dotsx, wide),
            None,
            probs,
            ds,
            pay,
            stat,
            head,
            i * (pay.shape[0] // PAIR),
        )


def sibling_mask(parents, core, half):
    steps = 2 * half // STEP_LEN
    reached = []
    for s in range(steps):
        bits = jnp.int32(1 << s)
        for t in range(s):
            bits = bits | jnp.where(parents[s] == t, reached[t], 0)
        reached.append(bits)

    def token(index):
        other_core = jnp.bitwise_xor((index // half) % 2, core)
        return other_core * (steps // 2) + (index % half) // STEP_LEN, index % STEP_LEN

    row_step, row_at = token(lax.broadcasted_iota(jnp.int32, (1, 2 * GROUP * half), 1))
    key_step, key_at = token(lax.broadcasted_iota(jnp.int32, (2 * half, 1), 0))
    row_bits = jnp.zeros(row_step.shape, jnp.int32)
    for s in range(steps):
        row_bits = jnp.where(row_step == s, reached[s], row_bits)
    seen = jnp.bitwise_and(jnp.right_shift(row_bits, key_step), 1) > 0
    return seen & ((key_step != row_step) | (key_at <= row_at))


def sibling_kernel(place, parents, q, qx, do, dox, dots, dotsx, ks, ksx, vs, vsx, probs, ds, pay, stat):
    kv = probs.shape[0]
    mask = sibling_mask(parents, place[1], ks.shape[0])
    for i in range(PAIR):
        head = pl.program_id(0) * PAIR + i
        wide = place[1] * kv + head
        at = head_columns(wide, D)
        attend(
            jnp.concatenate([ks[:, at], ksx[:, at]], axis=0),
            jnp.concatenate([vs[:, at], vsx[:, at]], axis=0),
            head_rows(q, qx, wide),
            head_rows(do, dox, wide),
            row_dots(dots, dotsx, wide),
            mask,
            probs,
            ds,
            pay,
            stat,
            head,
            i * (pay.shape[0] // PAIR),
        )


def merge_kernel(place, got, mine, out, weight):
    seq, core = place[0], place[1]
    sources = got.shape[0]
    at = pl.ds(pl.multiple_of((seq % (D // STEP_LEN)) * STEP_LEN, STEP_LEN), STEP_LEN)
    stats = got[:, CHUNK:, :].astype(f32)
    sib = mine[0, CHUNK:, :].astype(f32)
    sums = []
    for half in range(2):
        r = 3 * half
        reference, total = stats[:, r, :], stats[:, r + 1, :] + stats[:, r + 2, :]
        sib_reference, sib_total = sib[r : r + 1], sib[r + 1 : r + 2] + sib[r + 2 : r + 3]
        top = jnp.maximum(jnp.max(reference, axis=0, keepdims=True), sib_reference)
        row_total = jnp.sum(jnp.exp2(reference - top) * total, axis=0, keepdims=True) + jnp.exp2(sib_reference - top) * sib_total
        log_total = top + jnp.log2(row_total)
        weight[half] = jnp.concatenate(
            [
                SCALE * jnp.exp2(reference - log_total),
                SCALE * jnp.exp2(sib_reference - log_total),
                jnp.zeros((D - sources - 1, D), f32),
            ],
            axis=0,
        ).T
        weights = weight[half, at, :]
        rows = slice(half * STEP_LEN, (half + 1) * STEP_LEN)
        acc = weights[:, sources : sources + 1] * mine[0, rows, :].astype(f32)
        for i in range(sources):
            acc = acc + weights[:, i : i + 1] * got[i, rows, :].astype(f32)
        sums.append(acc)
    own, other = sums
    first = jnp.where(core == 0, own, other).astype(bf16)
    second = jnp.where(core == 0, other, own).astype(bf16)
    for i in range(sources):
        out[2 * i] = first
        out[2 * i + 1] = second


def key_grad_kernel(place, log_total, stat, probs, ds, q, qx, do, dox, grad_k, grad_v):
    kv = probs.shape[0]
    for i in range(PAIR):
        head = pl.program_id(0) * PAIR + i
        wide = place[1] * kv + head
        factor = jnp.exp2(stat[0, pl.ds(head, 1), :] - log_total[pl.ds(head, 1), :])
        factor = jnp.broadcast_to(factor, (D, factor.shape[1])).T
        q_rows = (head_rows(q, qx, wide).astype(f32) * (SCALE * factor)).astype(bf16)
        do_rows = (head_rows(do, dox, wide).astype(f32) * factor).astype(bf16)
        at = slice(i * D, (i + 1) * D)
        grad_k[:, at] = dot_nn(ds[head], q_rows).astype(bf16)
        grad_v[:, at] = dot_nn(probs[head], do_rows).astype(bf16)


def assemble_kernel(place, got, ks, ksx, vs, vsx, grad_q, grad_ks, grad_vs):
    kv, group, _, cores = got.shape[:4]
    for c in range(cores):
        for n in range(kv):
            for g in range(group):
                at = ((c * kv + n) * group + g) * D
                grad_q[:, at : at + D] = got[n, g, 0, c]
    width = ks.shape[1]

    @pl.when(place[1] == 0)
    def _():
        grad_ks[:, :width], grad_ks[:, width:] = ks[...], ksx[...]
        grad_vs[:, :width], grad_vs[:, width:] = vs[...], vsx[...]

    @pl.when(place[1] != 0)
    def _():
        grad_ks[:, :width], grad_ks[:, width:] = ksx[...], ks[...]
        grad_vs[:, :width], grad_vs[:, width:] = vsx[...], vs[...]


def combine(parts):
    top = functools.reduce(jnp.maximum, [x[0] for x in parts])
    return jnp.stack([top, sum(x[1] * jnp.exp2(x[0] - top) for x in parts)])


def total_over_seq(stat, size):
    stride = 1
    while stride < size:

        def moved(i, d):
            at = (i // stride) % RADIX
            return i + ((at + d) % RADIX - at) * stride

        others = [lax.ppermute(stat, "seq", [(i, moved(i, d)) for i in range(size)]) for d in range(1, RADIX)]
        stat = combine([stat] + others)
        stride *= RADIX
    return stat


def in_vmem(*arrays):
    return [pltpu.with_memory_space_constraint(x, pltpu.VMEM) for x in arrays]


def local(query, d_out, out_fwd, prompt_keys, prompt_value_rows, sibling_key_rows, sibling_value_rows, parents):
    seq, core = lax.axis_index("seq"), lax.axis_index("head")
    place = jnp.stack([seq, core]).astype(jnp.int32)
    devices = lax.axis_size("seq")
    kv = prompt_keys.shape[1] // D
    count = prompt_keys.shape[0]
    tokens = query.shape[0]
    rows = 2 * GROUP * tokens
    chunks = devices // kv
    blocks = tokens // STEP_LEN
    params = pltpu.CompilerParams(vmem_limit_bytes=VMEM_LIMIT, dimension_semantics=("arbitrary",))
    whole = pl.BlockSpec(memory_space=pltpu.VMEM)

    def swap(x):
        return lax.ppermute(x, "head", SWAP)

    qx, dox = swap(query), swap(d_out)
    dots = pl.pallas_call(
        out_dot_kernel,
        in_specs=[whole] * 2,
        out_specs=whole,
        out_shape=jax.ShapeDtypeStruct((query.shape[1] // D, tokens), f32),
        compiler_params=pltpu.CompilerParams(vmem_limit_bytes=VMEM_LIMIT),
        name="out_dot",
    )(d_out, out_fwd)
    dotsx = swap(dots)
    ksx, vsx = swap(sibling_key_rows), swap(sibling_value_rows)
    q_args = in_vmem(query, qx, d_out, dox)

    def attend_call(kernel, keys, prefetch, args, name):
        return pl.pallas_call(
            kernel,
            grid_spec=pltpu.PrefetchScalarGridSpec(
                num_scalar_prefetch=len(prefetch),
                grid=(kv // PAIR,),
                in_specs=[whole] * len(args),
                out_specs=[
                    whole,
                    whole,
                    pl.BlockSpec((chunks * PAIR, CHUNK + STAT_ROWS, D), lambda n, *_: (n, 0, 0)),
                    whole,
                ],
            ),
            out_shape=[
                pltpu.VMEM((kv, keys, rows), bf16),
                pltpu.VMEM((kv, keys, rows), bf16),
                jax.ShapeDtypeStruct((devices, CHUNK + STAT_ROWS, D), bf16),
                pltpu.VMEM((2, kv, rows), f32),
            ],
            compiler_params=params,
            cost_estimate=pl.CostEstimate(
                flops=6 * kv * keys * rows * D, bytes_accessed=4 * kv * keys * rows, transcendentals=kv * keys * rows
            ),
            name=name,
        )(*prefetch, *args)

    head_args = q_args + in_vmem(dots, dotsx)
    probs, ds, pay, stat = attend_call(
        prompt_kernel, count, (place,), head_args + in_vmem(prompt_keys, prompt_value_rows), "prompt"
    )
    got = lax.all_to_all(pay, "seq", split_axis=0, concat_axis=0, tiled=True)
    sib_probs, sib_ds, sib_pay, sib_stat = attend_call(
        sibling_kernel,
        2 * tokens,
        (place, parents),
        head_args + in_vmem(sibling_key_rows, ksx, sibling_value_rows, vsx),
        "sibling",
    )
    stats = combine([total_over_seq(stat, devices), sib_stat])
    log_total = stats[0] + jnp.log2(stats[1])

    merged = pl.pallas_call(
        merge_kernel,
        grid_spec=pltpu.PrefetchScalarGridSpec(
            num_scalar_prefetch=1,
            grid=(1,),
            in_specs=[
                pl.BlockSpec((devices, CHUNK + STAT_ROWS, D), lambda n, p: (0, 0, 0)),
                pl.BlockSpec((1, CHUNK + STAT_ROWS, D), lambda n, p: (p[0], 0, 0)),
            ],
            out_specs=pl.BlockSpec((2 * devices, STEP_LEN, D), lambda n, p: (0, 0, 0)),
            scratch_shapes=[pltpu.VMEM((2, D, D), f32)],
        ),
        out_shape=jax.ShapeDtypeStruct((2 * devices, STEP_LEN, D), bf16),
        compiler_params=params,
        name="merge",
    )(place, got, sib_pay)
    grad_q = lax.all_to_all(merged, ("seq", "head"), split_axis=0, concat_axis=0, tiled=True)

    def grad_call(keys, stat, probs, ds, name):
        return pl.pallas_call(
            key_grad_kernel,
            grid_spec=pltpu.PrefetchScalarGridSpec(
                num_scalar_prefetch=1,
                grid=(kv // PAIR,),
                in_specs=[whole] * 8,
                out_specs=[pl.BlockSpec((keys, PAIR * D), lambda n, *_: (0, n))] * 2,
            ),
            out_shape=[jax.ShapeDtypeStruct((keys, kv * D), bf16)] * 2,
            compiler_params=params,
            cost_estimate=pl.CostEstimate(
                flops=4 * kv * keys * rows * D, bytes_accessed=4 * kv * keys * rows, transcendentals=0
            ),
            name=name,
        )(place, *in_vmem(log_total, stat, probs, ds), *q_args)

    grad_ks, grad_vs = grad_call(2 * tokens, sib_stat, sib_probs, sib_ds, "sibling_grads")
    ks_other, vs_other = swap(grad_ks[tokens:]), swap(grad_vs[tokens:])
    grad_kp, grad_vp = grad_call(count, stat, probs, ds, "prompt_grads")

    half_spec = pl.BlockSpec((STEP_LEN, kv * D), lambda n, *_: (n, 0))
    grad_q, grad_ks, grad_vs = pl.pallas_call(
        assemble_kernel,
        grid_spec=pltpu.PrefetchScalarGridSpec(
            num_scalar_prefetch=1,
            grid=(blocks,),
            in_specs=[pl.BlockSpec((kv, GROUP, 1, 2, STEP_LEN, D), lambda n, *_: (0, 0, n, 0, 0, 0))] + [half_spec] * 4,
            out_specs=[
                pl.BlockSpec((STEP_LEN, query.shape[1]), lambda n, *_: (n, 0)),
                pl.BlockSpec((STEP_LEN, 2 * kv * D), lambda n, *_: (n, 0)),
                pl.BlockSpec((STEP_LEN, 2 * kv * D), lambda n, *_: (n, 0)),
            ],
        ),
        out_shape=[
            jax.ShapeDtypeStruct(query.shape, bf16),
            jax.ShapeDtypeStruct((tokens, 2 * kv * D), bf16),
            jax.ShapeDtypeStruct((tokens, 2 * kv * D), bf16),
        ],
        compiler_params=params,
        name="assemble",
    )(place, grad_q.reshape(kv, GROUP, blocks, 2, STEP_LEN, D), grad_ks, ks_other, grad_vs, vs_other)
    return grad_q, grad_kp, grad_vp, grad_ks, grad_vs


def solution(mesh):
    in_specs = (
        P("head", None),
        P("head", None),
        P("head", None),
        P("seq", "head"),
        P("seq", "head"),
        P("head", None),
        P("head", None),
        P(),
    )
    out_specs = (
        P("head", None),
        P("seq", "head"),
        P("seq", "head"),
        P("head", None),
        P("head", None),
    )
    return jax.shard_map(local, mesh=mesh, in_specs=in_specs, out_specs=out_specs, check_vma=False)
```

time: 1470 us -> 138 us (0.09)
  blocking collectives: 589 us -> 0 us
  local copies, waits for them, and re-layouts: 572 us -> 35 us
  starting transfers between devices: 138 us -> 34.8 us
  waiting for transfers between devices: 82.9 us -> 20.7 us
  matrix products: 58.4 us -> 0 us
  Pallas kernels: 0 us -> 45.1 us
  other arithmetic: 18.2 us -> 0.21 us
    gather x2 -> x0, local copies, waits for them, and re-layouts: 530 us -> none  [tree_mask(): reached[step_of[:, None], step_of[None, :]]]
    pmax x1 -> x0, blocking collectives: 295 us -> none  [local(): row_top = lax.pmax(local_top, 'seq')]
    psum x1 -> x0, blocking collectives: 286 us -> none  [local(): lax.psum(prompt_part + jnp.where(is_first, sib_part, 0.0), 'seq')]
    all_to_all x7 -> x2, starting transfers between devices: 138 us -> 18.8 us  [the longest x1 11.6 us: local(): got = lax.all_to_all(pay, 'seq', split_axis=0, concat_axis=0, tiled=True)]
    psum x1 -> x0, waiting for transfers between devices: 81.9 us -> none  [local(): grad_q = (score_scale * lax.psum(query_terms, 'seq')).astype(jnp.bfloat16)]
    dot_general x18 -> x0, matrix products: 58.4 us -> none  [the longest x1 9.44 us: local(): jnp.einsum('thgd,rhd->htgr', do_heads, vp_heads, preferred_element_type=f32)]
    pallas_call x0 -> x7, Pallas kernels: none -> 45.1 us  [the longest x2 24.3 us: attend_call(): pl.pallas_call(kernel, grid_spec=pltpu.PrefetchScalarGridSpec(num_scalar_...]
    ppermute x0 -> x16, waiting for transfers between devices: none -> 17.5 us  [the longest x9 16.7 us: total_over_seq(): lax.ppermute(stat, 'seq', [(i, moved(i, d)) for i in range(size)])]
  transfers between devices with their start and end apart: 8 -> 18, of which waited for: 2 -> 7; matrix products, arithmetic and copies ran while one was open for 39% -> 0% of each run, Pallas kernels for 0% -> 15%
where the time goes in v1:
time: 138 us; the launch traced here: 137 us
  Pallas kernels  45.1 us (33%)
  local copies, waits for them, and re-layouts  35 us (25%)
  starting transfers between devices  34.8 us (25%)
  waiting for transfers between devices  20.7 us (15%)
    unnamed x54, local copies, waits for them, and re-layouts  35 us
    pallas_call x2, Pallas kernels, attend_call(): pl.pallas_call(kernel, grid_spec=pltpu.PrefetchScalarGridSpec(num_scalar_...  24.3 us
    ppermute x9, waiting for transfers between devices, total_over_seq(): lax.ppermute(stat, 'seq', [(i, moved(i, d)) for i in range(size)])  16.7 us
    pallas_call x2, Pallas kernels, grad_call(): pl.pallas_call(key_grad_kernel, grid_spec=pltpu.PrefetchScalarGridSpec(nu...  12.4 us
    all_to_all x1, starting transfers between devices, local(): got = lax.all_to_all(pay, 'seq', split_axis=0, concat_axis=0, tiled=True)  11.6 us
    ppermute x9, starting transfers between devices, total_over_seq(): lax.ppermute(stat, 'seq', [(i, moved(i, d)) for i in range(size)])  11 us
    all_to_all x1, starting transfers between devices, local(): lax.all_to_all(merged, ('seq', 'head'), split_axis=0, concat_axis=0, tile...  7.21 us
    ppermute x7, starting transfers between devices, swap(): return lax.ppermute(x, 'head', SWAP)  5 us
  transfers between devices with their start and end apart: 18, of which 7 were waited for; matrix products, arithmetic and copies ran while one was open for 0% of the time, Pallas kernels for 15%

profile of v1, /device:TPU:1, one launch (start us, length us, event | category | flops | bytes accessed | tf_op | source)
XLA Modules:
  0.0 136.7 jit_solution(15879354097814418415)
XLA Ops:
  0.6 1.5 %collective-permute-start = (bf16[128,4096]{1,0:T(8,128)(2,1)}, bf16[128,4096]{1,0:T(8,128)(2,1)S(1)}, u32[]{:S(2)}, u32[]{:S(2)}) collective-permute-start(bf16[128,4096]{1,0:T(8,128)(2,1)} %q.7), channel_id=1, source_target_pairs={{0,1},{1,0},{2,3},{3,2},{4,5},{5,4},{6,7},{7,6},{8,9},{9,8},{10,11... | collective-permute-start | bytes 3145736 | tf_op jit(solution)/shard_map/ppermute | solution.py:290
  2.1 0.1 collective-permute-start.1
  2.2 1.2 copy-done
  3.5 1.2 copy-done.19
  4.7 1.2 out_dot.1.dots
  5.9 0.4 collective-permute-start.2
  6.3 0.1 pad_add_fusion.place
  6.4 0.8 collective-permute-done.2.dotsx
  7.2 0.0 copy-start.25
  7.2 1.6 %copy-done.25 = bf16[1024,1024]{1,0:T(8,128)(2,1)S(1)} copy-done((bf16[1024,1024]{1,0:T(8,128)(2,1)S(1)}, bf16[1024,1024]{1,0:T(8,128)(2,1)}, u32[]{:S(2)}) %copy-start.25) | copy-done | bytes 2097176
  8.8 1.6 %copy-done.26 = bf16[1024,1024]{1,0:T(8,128)(2,1)S(1)} copy-done((bf16[1024,1024]{1,0:T(8,128)(2,1)S(1)}, bf16[1024,1024]{1,0:T(8,128)(2,1)}, u32[]{:S(2)}) %copy-start.26) | copy-done | bytes 2097176
  10.4 17.3 %prompt.1 = (bf16[8,1024,512]{2,1,0:T(8,128)(2,1)S(1)}, bf16[8,1024,512]{2,1,0:T(8,128)(2,1)S(1)}, bf16[64,80,128]{2,1,0:T(8,128)(2,1)S(1)}, f32[2,8,512]{2,1,0:T(8,128)S(1)}) custom-call(s32[2]{0:T(128)S(1)} %pad_add_fusion.place, bf16[128,4096]{1,0:T(8,128)(2,1)S(1)} %copy-done.2, bf16[128,4096]{1,0:T(8,128)(2,1)S(1)} %collective-permute-done.qx, ...), custom_call_target="tpu_custom_call" | custom-call | flops 3221225472 | bytes 16777216 | tf_op jit(solution)/shard_map/prompt/pallas_call | solution.py:306
  27.6 3.3 %copy-done.3 = bf16[8,1024,512]{2,1,0:T(8,128)(2,1)} copy-done((bf16[8,1024,512]{2,1,0:T(8,128)(2,1)}, bf16[8,1024,512]{2,1,0:T(8,128)(2,1)S(1)}, u32[]{:S(2)}) %copy-start.3) | copy-done | bytes 8388632
  30.9 3.3 %copy-done.5 = bf16[8,1024,512]{2,1,0:T(8,128)(2,1)} copy-done((bf16[8,1024,512]{2,1,0:T(8,128)(2,1)}, bf16[8,1024,512]{2,1,0:T(8,128)(2,1)S(1)}, u32[]{:S(2)}) %copy-start.5) | copy-done | bytes 8388632
  34.2 1.1 copy-done.12
  35.3 11.6 %all-to-all-start = ((bf16[64,80,128]{2,1,0:T(8,128)(2,1)}), bf16[64,80,128]{2,1,0:T(8,128)(2,1)}, u32[]{:S(2)}, u32[]{:S(2)}) async-start(bf16[64,80,128]{2,1,0:T(8,128)(2,1)} %copy-done.12), calls=%async_computation | async-start | bytes 2621440 | tf_op jit(solution)/shard_map/all_to_all | solution.py:336
  46.9 0.7 collective-permute-start.3
  47.6 0.1 collective-permute-start.4
  47.7 2.4 %collective-permute-start.7 = (f32[2,8,512]{2,1,0:T(8,128)S(1)}, f32[2,8,512]{2,1,0:T(8,128)S(1)}, u32[]{:S(2)}, u32[]{:S(2)}) collective-permute-start(f32[2,8,512]{2,1,0:T(8,128)S(1)} %get-tuple-element.22.stat), channel_id=1, source_target_pairs={{0,6},{2,0},{4,2},{6,4},{8,14},{10,8},{12,10},{14,12},{16,22},{18,... | collective-permute-start | bytes 98312 | tf_op jit(solution)/shard_map/ppermute | solution.py:266
  50.1 0.6 collective-permute-start.6
  50.7 0.6 collective-permute-start.5
  51.3 0.0 collective-permute-done.3.ksx
  51.3 0.0 copy-start.20
  51.3 1.0 copy-done.20
  52.3 1.0 copy-done.21
  53.4 7.0 %sibling.1 = (bf16[8,256,512]{2,1,0:T(8,128)(2,1)S(1)}, bf16[8,256,512]{2,1,0:T(8,128)(2,1)S(1)}, bf16[64,80,128]{2,1,0:T(8,128)(2,1)S(1)}, f32[2,8,512]{2,1,0:T(8,128)S(1)}) custom-call(s32[2]{0:T(128)S(1)} %pad_add_fusion.place, s32[8]{0:T(128)S(1)} %copy-done.24, bf16[128,4096]{1,0:T(8,128)(2,1)S(1)} %copy-done.2, ...), custom_call_target="tpu_custom_call" | custom-call | flops 805306368 | bytes 4194304 | tf_op jit(solution)/shard_map/sibling/pallas_call | solution.py:306
  60.4 0.0 copy-start.8
  60.4 1.3 copy-done.8
  61.7 1.3 copy-done.10
  63.0 1.1 copy-done.13
  64.1 3.2 %all-to-all-done.got = bf16[64,80,128]{2,1,0:T(8,128)(2,1)} async-done(((bf16[64,80,128]{2,1,0:T(8,128)(2,1)}), bf16[64,80,128]{2,1,0:T(8,128)(2,1)}, u32[]{:S(2)}, u32[]{:S(2)}) %all-to-all-start) | async-done | bytes 1310752 | tf_op jit(solution)/shard_map/all_to_all | solution.py:336
  67.3 1.3 copy-done.14
  68.7 3.0 %merge.1 = bf16[128,32,128]{2,1,0:T(8,128)(2,1)S(1)} custom-call(s32[2]{0:T(128)S(1)} %pad_add_fusion.place, bf16[64,80,128]{2,1,0:T(8,128)(2,1)} %all-to-all-done.got, bf16[64,80,128]{2,1,0:T(8,128)(2,1)S(1)} %copy-done.14), custom_call_target="tpu_custom_call" | custom-call | tf_op jit(solution)/shard_map/merge/pallas_call | solution.py:347
  71.7 0.0 copy-start.7
  71.7 1.0 copy-done.7
  72.7 7.2 %all-to-all-start.1 = ((bf16[128,32,128]{2,1,0:T(8,128)(2,1)}), bf16[128,32,128]{2,1,0:T(8,128)(2,1)}, u32[]{:S(2)}, u32[]{:S(2)}) async-start(bf16[128,32,128]{2,1,0:T(8,128)(2,1)} %copy-done.7), calls=%async_computation.1 | async-start | bytes 2097152 | tf_op jit(solution)/shard_map/all_to_all | solution.py:363
  79.9 3.5 %collective-permute-start.10 = (f32[2,8,512]{2,1,0:T(8,128)S(1)}, f32[2,8,512]{2,1,0:T(8,128)S(1)}, u32[]{:S(2)}, u32[]{:S(2)}) collective-permute-start(f32[2,8,512]{2,1,0:T(8,128)S(1)} %pad_maximum_fusion), channel_id=1, source_target_pairs={{0,24},{2,26},{4,28},{6,30},{8,0},{10,2},{12,4},{14,6},{16,8},{18,... | collective-permute-start | bytes 98312 | tf_op jit(solution)/shard_map/ppermute | solution.py:266
  83.3 0.1 collective-permute-start.9
  83.5 0.8 collective-permute-start.8
  84.2 1.2 collective-permute-done.10
  85.4 9.2 %collective-permute-done.9 = f32[2,8,512]{2,1,0:T(8,128)S(1)} collective-permute-done((f32[2,8,512]{2,1,0:T(8,128)S(1)}, f32[2,8,512]{2,1,0:T(8,128)S(1)}, u32[]{:S(2)}, u32[]{:S(2)}) %collective-permute-start.9) | collective-permute-done | bytes 32800 | tf_op jit(solution)/shard_map/ppermute | solution.py:266
  94.6 2.4 %collective-permute-done.8 = f32[2,8,512]{2,1,0:T(8,128)S(1)} collective-permute-done((f32[2,8,512]{2,1,0:T(8,128)S(1)}, f32[2,8,512]{2,1,0:T(8,128)S(1)}, u32[]{:S(2)}, u32[]{:S(2)}) %collective-permute-start.8) | collective-permute-done | bytes 32800 | tf_op jit(solution)/shard_map/ppermute | solution.py:266
  97.0 1.8 %collective-permute-start.13 = (f32[2,8,512]{2,1,0:T(8,128)S(1)}, f32[2,8,512]{2,1,0:T(8,128)S(1)}, u32[]{:S(2)}, u32[]{:S(2)}) collective-permute-start(f32[2,8,512]{2,1,0:T(8,128)S(1)} %pad_maximum_fusion.1), channel_id=1, source_target_pairs={{0,96},{2,98},{4,100},{6,102},{8,104},{10,106},{12,108},{14,110},{... | collective-permute-start | bytes 98312 | tf_op jit(solution)/shard_map/ppermute | solution.py:266
  98.8 1.2 collective-permute-start.12
  100.1 0.0 collective-permute-start.11
  100.1 3.0 %collective-permute-done.12 = f32[2,8,512]{2,1,0:T(8,128)S(1)} collective-permute-done((f32[2,8,512]{2,1,0:T(8,128)S(1)}, f32[2,8,512]{2,1,0:T(8,128)S(1)}, u32[]{:S(2)}, u32[]{:S(2)}) %collective-permute-start.12) | collective-permute-done | bytes 32800 | tf_op jit(solution)/shard_map/ppermute | solution.py:266
  103.1 0.9 collective-permute-done.11
  104.0 0.1 fusion.6.log_total
  104.1 0.0 copy-start.9
  104.1 1.6 %copy-done.9 = bf16[8,256,512]{2,1,0:T(8,128)(2,1)S(1)} copy-done((bf16[8,256,512]{2,1,0:T(8,128)(2,1)S(1)}, bf16[8,256,512]{2,1,0:T(8,128)(2,1)}, u32[]{:S(2)}) %copy-start.9) | copy-done | bytes 2097176
  105.7 1.6 %copy-done.11 = bf16[8,256,512]{2,1,0:T(8,128)(2,1)S(1)} copy-done((bf16[8,256,512]{2,1,0:T(8,128)(2,1)S(1)}, bf16[8,256,512]{2,1,0:T(8,128)(2,1)}, u32[]{:S(2)}) %copy-start.11) | copy-done | bytes 2097176
  107.3 4.2 %sibling_grads.1 = (bf16[256,1024]{1,0:T(8,128)(2,1)S(1)}, bf16[256,1024]{1,0:T(8,128)(2,1)S(1)}) custom-call(s32[2]{0:T(128)S(1)} %pad_add_fusion.place, f32[8,512]{1,0:T(8,128)S(1)} %fusion.6.log_total, f32[2,8,512]{2,1,0:T(8,128)S(1)} %get-tuple-element.23.stat, bf16[8,256,512]{2,1,0:T(8,128)(2,1)S(1)} %copy-done.9, bf16[8,256,512]{2,1,0:T(8,128)(2,1)S(1)} %copy-done.11, ...), custom_call_target="tpu_custom_call" | custom-call | flops 536870912 | bytes 4194304 | tf_op jit(solution)/shard_map/sibling_grads/pallas_call | solution.py:366
  111.5 0.0 copy-start.15
  111.5 0.0 copy-start.17
  111.5 2.1 %collective-permute-start.14 = (bf16[128,1024]{1,0:T(8,128)(2,1)S(1)}, bf16[128,1024]{1,0:T(8,128)(2,1)S(1)}, u32[]{:S(2)}, u32[]{:S(2)}) collective-permute-start(bf16[128,1024]{1,0:T(8,128)(2,1)S(1)} %slice.105), channel_id=1, source_target_pairs={{0,1},{1,0},{2,3},{3,2},{4,5},{5,4},{6,7},{7,6},{8,9},{9,8},{10,11... | collective-permute-start | bytes 786440 | tf_op jit(solution)/shard_map/ppermute | solution.py:290
  113.6 0.1 collective-permute-start.15
  113.8 3.4 %copy-done.4 = bf16[8,1024,512]{2,1,0:T(8,128)(2,1)S(1)} copy-done((bf16[8,1024,512]{2,1,0:T(8,128)(2,1)S(1)}, bf16[8,1024,512]{2,1,0:T(8,128)(2,1)}, u32[]{:S(2)}) %copy-start.4) | copy-done | bytes 8388632
  117.1 3.4 %copy-done.6 = bf16[8,1024,512]{2,1,0:T(8,128)(2,1)S(1)} copy-done((bf16[8,1024,512]{2,1,0:T(8,128)(2,1)S(1)}, bf16[8,1024,512]{2,1,0:T(8,128)(2,1)}, u32[]{:S(2)}) %copy-start.6) | copy-done | bytes 8388632
  120.5 8.2 %prompt_grads.1 = (bf16[1024,1024]{1,0:T(8,128)(2,1)}, bf16[1024,1024]{1,0:T(8,128)(2,1)}) custom-call(s32[2]{0:T(128)S(1)} %pad_add_fusion.place, f32[8,512]{1,0:T(8,128)S(1)} %fusion.6.log_total, f32[2,8,512]{2,1,0:T(8,128)S(1)} %get-tuple-element.22.stat, bf16[8,1024,512]{2,1,0:T(8,128)(2,1)S(1)} %copy-done.4, bf16[8,1024,512]{2,1,0:T(8,128)(2,1)S(1)} %copy-done.6, ...), custom_call_target="tpu_custom_call" | custom-call | flops 2147483648 | bytes 16777216 | tf_op jit(solution)/shard_map/prompt_grads/pallas_call | solution.py:366
  128.8 0.7 copy-done.22
  129.5 1.0 copy-done.16
  130.5 1.0 copy-done.18
  131.6 0.9 copy-done.23
  132.5 4.2 %assemble.1 = (bf16[128,4096]{1,0:T(8,128)(2,1)}, bf16[128,2048]{1,0:T(8,128)(2,1)}, bf16[128,2048]{1,0:T(8,128)(2,1)}) custom-call(s32[2]{0:T(128)S(1)} %pad_add_fusion.place, bf16[8,2,4,2,32,128]{5,4,3,2,1,0:T(8,128)(2,1)} %bitcast.2.got, bf16[256,1024]{1,0:T(8,128)(2,1)S(1)} %copy-done.16, bf16[128,1024]{1,0:T(8,128)(2,1)S(1)} %collective-permute-done.14.ksx, ...), custom_call_target="tpu_custom_call" | custom-call | tf_op jit(solution)/shard_map/assemble/pallas_call | solution.py:387
  (41 shorter events, 0.2 us)
Async XLA Ops:
  0.6 6.5 %collective-permute-start = (bf16[128,4096]{1,0:T(8,128)(2,1)}, bf16[128,4096]{1,0:T(8,128)(2,1)S(1)}, u32[]{:S(2)}, u32[]{:S(2)}) collective-permute-start(bf16[128,4096]{1,0:T(8,128)(2,1)} %q.7), channel_id=1, source_target_pairs={{0,1},{1,0},{2,3},{3,2},{4,5},{5,4},{6,7},{7,6},{8,9},{9,8},{10,11... | collective-permute-start | bytes 3145736 | tf_op jit(solution)/shard_map/ppermute | solution.py:290
  2.1 5.0 %collective-permute-start.1 = (bf16[128,4096]{1,0:T(8,128)(2,1)}, bf16[128,4096]{1,0:T(8,128)(2,1)}, u32[]{:S(2)}, u32[]{:S(2)}) collective-permute-start(bf16[128,4096]{1,0:T(8,128)(2,1)} %do.9), channel_id=1, source_target_pairs={{0,1},{1,0},{2,3},{3,2},{4,5},{5,4},{6,7},{7,6},{8,9},{9,8},{10,11... | collective-permute-start | bytes 3145736 | tf_op jit(solution)/shard_map/ppermute | solution.py:290
  2.2 1.2 copy-start
  3.5 1.2 copy-start.19
  4.7 2.5 %copy-start.1 = (bf16[128,4096]{1,0:T(8,128)(2,1)S(1)}, bf16[128,4096]{1,0:T(8,128)(2,1)}, u32[]{:S(2)}) copy-start(bf16[128,4096]{1,0:T(8,128)(2,1)} %do.9) | copy-start | bytes 3145732
  4.7 2.5 %copy-start.2 = (bf16[128,4096]{1,0:T(8,128)(2,1)S(1)}, bf16[128,4096]{1,0:T(8,128)(2,1)}, u32[]{:S(2)}) copy-start(bf16[128,4096]{1,0:T(8,128)(2,1)} %q.7) | copy-start | bytes 3145732
  5.9 1.3 collective-permute-start.2
  7.2 1.6 %copy-start.25 = (bf16[1024,1024]{1,0:T(8,128)(2,1)S(1)}, bf16[1024,1024]{1,0:T(8,128)(2,1)}, u32[]{:S(2)}) copy-start(bf16[1024,1024]{1,0:T(8,128)(2,1)} %kp.1) | copy-start | bytes 6291460
  8.8 1.6 %copy-start.26 = (bf16[1024,1024]{1,0:T(8,128)(2,1)S(1)}, bf16[1024,1024]{1,0:T(8,128)(2,1)}, u32[]{:S(2)}) copy-start(bf16[1024,1024]{1,0:T(8,128)(2,1)} %vp.1) | copy-start | bytes 6291460
  27.6 3.3 %copy-start.3 = (bf16[8,1024,512]{2,1,0:T(8,128)(2,1)}, bf16[8,1024,512]{2,1,0:T(8,128)(2,1)S(1)}, u32[]{:S(2)}) copy-start(bf16[8,1024,512]{2,1,0:T(8,128)(2,1)S(1)} %get-tuple-element.29.probs) | copy-start | bytes 25165828
  30.9 3.3 %copy-start.5 = (bf16[8,1024,512]{2,1,0:T(8,128)(2,1)}, bf16[8,1024,512]{2,1,0:T(8,128)(2,1)S(1)}, u32[]{:S(2)}) copy-start(bf16[8,1024,512]{2,1,0:T(8,128)(2,1)S(1)} %get-tuple-element.30.ds) | copy-start | bytes 25165828
  34.2 1.1 copy-start.12
  35.3 16.0 %copy-start.24 = (s32[8]{0:T(128)S(1)}, s32[8]{0:T(128)}, u32[]{:S(2)}) copy-start(s32[8]{0:T(128)} %parents.1) | copy-start | bytes 100
  35.3 32.1 %all-to-all-start = ((bf16[64,80,128]{2,1,0:T(8,128)(2,1)}), bf16[64,80,128]{2,1,0:T(8,128)(2,1)}, u32[]{:S(2)}, u32[]{:S(2)}) async-start(bf16[64,80,128]{2,1,0:T(8,128)(2,1)} %copy-done.12), calls=%async_computation | async-start | bytes 2621440 | tf_op jit(solution)/shard_map/all_to_all | solution.py:336
  46.9 4.4 %collective-permute-start.3 = (bf16[128,2048]{1,0:T(8,128)(2,1)}, bf16[128,2048]{1,0:T(8,128)(2,1)S(1)}, u32[]{:S(2)}, u32[]{:S(2)}) collective-permute-start(bf16[128,2048]{1,0:T(8,128)(2,1)} %ks.1), channel_id=1, source_target_pairs={{0,1},{1,0},{2,3},{3,2},{4,5},{5,4},{6,7},{7,6},{8,9},{9,8},{10,11... | collective-permute-start | bytes 1572872 | tf_op jit(solution)/shard_map/ppermute | solution.py:290
  47.6 3.7 %collective-permute-start.4 = (bf16[128,2048]{1,0:T(8,128)(2,1)}, bf16[128,2048]{1,0:T(8,128)(2,1)S(1)}, u32[]{:S(2)}, u32[]{:S(2)}) collective-permute-start(bf16[128,2048]{1,0:T(8,128)(2,1)} %vs.1), channel_id=1, source_target_pairs={{0,1},{1,0},{2,3},{3,2},{4,5},{5,4},{6,7},{7,6},{8,9},{9,8},{10,11... | collective-permute-start | bytes 1572872 | tf_op jit(solution)/shard_map/ppermute | solution.py:290
  47.7 16.4 %collective-permute-start.7 = (f32[2,8,512]{2,1,0:T(8,128)S(1)}, f32[2,8,512]{2,1,0:T(8,128)S(1)}, u32[]{:S(2)}, u32[]{:S(2)}) collective-permute-start(f32[2,8,512]{2,1,0:T(8,128)S(1)} %get-tuple-element.22.stat), channel_id=1, source_target_pairs={{0,6},{2,0},{4,2},{6,4},{8,14},{10,8},{12,10},{14,12},{16,22},{18,... | collective-permute-start | bytes 98312 | tf_op jit(solution)/shard_map/ppermute | solution.py:266
  50.1 14.0 %collective-permute-start.6 = (f32[2,8,512]{2,1,0:T(8,128)S(1)}, f32[2,8,512]{2,1,0:T(8,128)S(1)}, u32[]{:S(2)}, u32[]{:S(2)}) collective-permute-start(f32[2,8,512]{2,1,0:T(8,128)S(1)} %get-tuple-element.22.stat), channel_id=1, source_target_pairs={{0,4},{2,6},{4,0},{6,2},{8,12},{10,14},{12,8},{14,10},{16,20},{18,... | collective-permute-start | bytes 98312 | tf_op jit(solution)/shard_map/ppermute | solution.py:266
  50.7 13.4 %collective-permute-start.5 = (f32[2,8,512]{2,1,0:T(8,128)S(1)}, f32[2,8,512]{2,1,0:T(8,128)S(1)}, u32[]{:S(2)}, u32[]{:S(2)}) collective-permute-start(f32[2,8,512]{2,1,0:T(8,128)S(1)} %get-tuple-element.22.stat), channel_id=1, source_target_pairs={{0,2},{2,4},{4,6},{6,0},{8,10},{10,12},{12,14},{14,8},{16,18},{18,... | collective-permute-start | bytes 98312 | tf_op jit(solution)/shard_map/ppermute | solution.py:266
  51.3 1.0 copy-start.20
  52.3 1.0 copy-start.21
  60.4 1.3 copy-start.8
  61.7 1.3 copy-start.10
  63.0 1.1 copy-start.13
  67.3 1.3 copy-start.14
  71.7 1.0 copy-start.7
  72.7 56.8 %all-to-all-start.1 = ((bf16[128,32,128]{2,1,0:T(8,128)(2,1)}), bf16[128,32,128]{2,1,0:T(8,128)(2,1)}, u32[]{:S(2)}, u32[]{:S(2)}) async-start(bf16[128,32,128]{2,1,0:T(8,128)(2,1)} %copy-done.7), calls=%async_computation.1 | async-start | bytes 2097152 | tf_op jit(solution)/shard_map/all_to_all | solution.py:363
  79.9 5.6 %collective-permute-start.10 = (f32[2,8,512]{2,1,0:T(8,128)S(1)}, f32[2,8,512]{2,1,0:T(8,128)S(1)}, u32[]{:S(2)}, u32[]{:S(2)}) collective-permute-start(f32[2,8,512]{2,1,0:T(8,128)S(1)} %pad_maximum_fusion), channel_id=1, source_target_pairs={{0,24},{2,26},{4,28},{6,30},{8,0},{10,2},{12,4},{14,6},{16,8},{18,... | collective-permute-start | bytes 98312 | tf_op jit(solution)/shard_map/ppermute | solution.py:266
  83.3 11.3 %collective-permute-start.9 = (f32[2,8,512]{2,1,0:T(8,128)S(1)}, f32[2,8,512]{2,1,0:T(8,128)S(1)}, u32[]{:S(2)}, u32[]{:S(2)}) collective-permute-start(f32[2,8,512]{2,1,0:T(8,128)S(1)} %pad_maximum_fusion), channel_id=1, source_target_pairs={{0,16},{2,18},{4,20},{6,22},{8,24},{10,26},{12,28},{14,30},{16,0},... | collective-permute-start | bytes 98312 | tf_op jit(solution)/shard_map/ppermute | solution.py:266
  83.5 13.5 %collective-permute-start.8 = (f32[2,8,512]{2,1,0:T(8,128)S(1)}, f32[2,8,512]{2,1,0:T(8,128)S(1)}, u32[]{:S(2)}, u32[]{:S(2)}) collective-permute-start(f32[2,8,512]{2,1,0:T(8,128)S(1)} %pad_maximum_fusion), channel_id=1, source_target_pairs={{0,8},{2,10},{4,12},{6,14},{8,16},{10,18},{12,20},{14,22},{16,24},... | collective-permute-start | bytes 98312 | tf_op jit(solution)/shard_map/ppermute | solution.py:266
  97.0 3.1 %collective-permute-start.13 = (f32[2,8,512]{2,1,0:T(8,128)S(1)}, f32[2,8,512]{2,1,0:T(8,128)S(1)}, u32[]{:S(2)}, u32[]{:S(2)}) collective-permute-start(f32[2,8,512]{2,1,0:T(8,128)S(1)} %pad_maximum_fusion.1), channel_id=1, source_target_pairs={{0,96},{2,98},{4,100},{6,102},{8,104},{10,106},{12,108},{14,110},{... | collective-permute-start | bytes 98312 | tf_op jit(solution)/shard_map/ppermute | solution.py:266
  98.8 4.3 %collective-permute-start.12 = (f32[2,8,512]{2,1,0:T(8,128)S(1)}, f32[2,8,512]{2,1,0:T(8,128)S(1)}, u32[]{:S(2)}, u32[]{:S(2)}) collective-permute-start(f32[2,8,512]{2,1,0:T(8,128)S(1)} %pad_maximum_fusion.1), channel_id=1, source_target_pairs={{0,64},{2,66},{4,68},{6,70},{8,72},{10,74},{12,76},{14,78},{16,80}... | collective-permute-start | bytes 98312 | tf_op jit(solution)/shard_map/ppermute | solution.py:266
  100.1 4.0 %collective-permute-start.11 = (f32[2,8,512]{2,1,0:T(8,128)S(1)}, f32[2,8,512]{2,1,0:T(8,128)S(1)}, u32[]{:S(2)}, u32[]{:S(2)}) collective-permute-start(f32[2,8,512]{2,1,0:T(8,128)S(1)} %pad_maximum_fusion.1), channel_id=1, source_target_pairs={{0,32},{2,34},{4,36},{6,38},{8,40},{10,42},{12,44},{14,46},{16,48}... | collective-permute-start | bytes 98312 | tf_op jit(solution)/shard_map/ppermute | solution.py:266
  104.1 1.6 %copy-start.9 = (bf16[8,256,512]{2,1,0:T(8,128)(2,1)S(1)}, bf16[8,256,512]{2,1,0:T(8,128)(2,1)}, u32[]{:S(2)}) copy-start(bf16[8,256,512]{2,1,0:T(8,128)(2,1)} %copy-done.8) | copy-start | bytes 6291460
  105.7 1.6 %copy-start.11 = (bf16[8,256,512]{2,1,0:T(8,128)(2,1)S(1)}, bf16[8,256,512]{2,1,0:T(8,128)(2,1)}, u32[]{:S(2)}) copy-start(bf16[8,256,512]{2,1,0:T(8,128)(2,1)} %copy-done.10) | copy-start | bytes 6291460
  111.5 2.2 %copy-start.15 = (bf16[256,1024]{1,0:T(8,128)(2,1)}, bf16[256,1024]{1,0:T(8,128)(2,1)S(1)}, u32[]{:S(2)}) copy-start(bf16[256,1024]{1,0:T(8,128)(2,1)S(1)} %get-tuple-element.26.ks) | copy-start | bytes 1572868
  111.5 2.2 %copy-start.17 = (bf16[256,1024]{1,0:T(8,128)(2,1)}, bf16[256,1024]{1,0:T(8,128)(2,1)S(1)}, u32[]{:S(2)}) copy-start(bf16[256,1024]{1,0:T(8,128)(2,1)S(1)} %get-tuple-element.27.vs) | copy-start | bytes 1572868
  111.5 17.2 %collective-permute-start.14 = (bf16[128,1024]{1,0:T(8,128)(2,1)S(1)}, bf16[128,1024]{1,0:T(8,128)(2,1)S(1)}, u32[]{:S(2)}, u32[]{:S(2)}) collective-permute-start(bf16[128,1024]{1,0:T(8,128)(2,1)S(1)} %slice.105), channel_id=1, source_target_pairs={{0,1},{1,0},{2,3},{3,2},{4,5},{5,4},{6,7},{7,6},{8,9},{9,8},{10,11... | collective-permute-start | bytes 786440 | tf_op jit(solution)/shard_map/ppermute | solution.py:290
  113.6 15.1 %collective-permute-start.15 = (bf16[128,1024]{1,0:T(8,128)(2,1)S(1)}, bf16[128,1024]{1,0:T(8,128)(2,1)S(1)}, u32[]{:S(2)}, u32[]{:S(2)}) collective-permute-start(bf16[128,1024]{1,0:T(8,128)(2,1)S(1)} %slice.106), channel_id=1, source_target_pairs={{0,1},{1,0},{2,3},{3,2},{4,5},{5,4},{6,7},{7,6},{8,9},{9,8},{10,11... | collective-permute-start | bytes 786440 | tf_op jit(solution)/shard_map/ppermute | solution.py:290
  113.7 3.4 %copy-start.4 = (bf16[8,1024,512]{2,1,0:T(8,128)(2,1)S(1)}, bf16[8,1024,512]{2,1,0:T(8,128)(2,1)}, u32[]{:S(2)}) copy-start(bf16[8,1024,512]{2,1,0:T(8,128)(2,1)} %copy-done.3) | copy-start | bytes 25165828
  117.1 3.4 %copy-start.6 = (bf16[8,1024,512]{2,1,0:T(8,128)(2,1)S(1)}, bf16[8,1024,512]{2,1,0:T(8,128)(2,1)}, u32[]{:S(2)}) copy-start(bf16[8,1024,512]{2,1,0:T(8,128)(2,1)} %copy-done.5) | copy-start | bytes 25165828
  128.8 0.7 copy-start.22
  129.5 1.0 copy-start.16
  130.5 1.0 copy-start.18
  131.5 0.9 copy-start.23

commit v2 on v1

v2 whole, which is shorter than its diff:
```python
import functools
import math

import jax
import jax.numpy as jnp
from jax import lax
from jax.experimental import pallas as pl
from jax.experimental.pallas import tpu as pltpu
from jax.sharding import PartitionSpec as P

f32 = jnp.float32
bf16 = jnp.bfloat16

D = 128
GROUP = 2
STEP_LEN = 32
SCALE = 144.0 ** (-0.5)
SCALE2 = SCALE * math.log2(math.e)
MASKED = -1e30
TOTAL_LOW, TOTAL_HIGH = 2.0**-60, 2.0**60
SWAP = [(0, 1), (1, 0)]
RADIX = 4
PAIR = 2
VMEM_LIMIT = 20 * 1024 * 1024

CHUNK = 2 * STEP_LEN
STAT_ROWS = 16


def dot_nt(a, b):
    return lax.dot_general(a, b, (((1,), (1,)), ((), ())), preferred_element_type=f32)


def dot_tn(a, b):
    return lax.dot_general(a, b, (((0,), (0,)), ((), ())), preferred_element_type=f32)


def dot_nn(a, b):
    return jnp.dot(a, b, preferred_element_type=f32)


def fold8(x, op):
    return op(x.reshape(x.shape[0] // 8, 8, x.shape[1]), axis=0)


def head_rows(own, other, i):
    cols = [slice((GROUP * i + g) * D, (GROUP * i + g + 1) * D) for g in range(GROUP)]
    return jnp.concatenate([x[:, at] for at in cols for x in (own, other)], axis=0)


def out_dot_kernel(do, o, out):
    ones = jnp.ones((8, D), bf16)
    for head in range(out.shape[0]):
        at = slice(head * D, (head + 1) * D)
        product = do[:, at].astype(f32) * o[:, at].astype(f32)
        high = product.astype(bf16)
        low = (product - high.astype(f32)).astype(bf16)
        out[head : head + 1, :] = (dot_nt(ones, high) + dot_nt(ones, low))[0:1]


def attend(keys, values, q_rows, do_rows, out_dot, mask, pay_ref, stat_ref, head, k0):
    rows = q_rows.shape[0]

    def masked(scores):
        return scores if mask is None else jnp.where(mask, scores, MASKED)

    def run(reference):
        scores = masked(dot_nt(keys, q_rows)) * SCALE2
        probs = jnp.exp2(scores if reference is None else scores - reference)
        dscores = (probs * (dot_nt(values, do_rows) - out_dot)).astype(bf16)
        total = jnp.sum(fold8(probs, jnp.sum), axis=0, keepdims=True)
        grad = dot_tn(keys, dscores).T.astype(bf16)
        held = jnp.zeros((1, rows), f32) if reference is None else reference
        stat_ref[0, pl.ds(head, 1), :] = held
        stat_ref[1, pl.ds(head, 1), :] = total
        high = total.astype(bf16).astype(f32)
        stats = [held, high, total - high]
        for g in range(GROUP):
            own, other = g * 2 * D, (g * 2 + 1) * D
            parts = [x[:, at : at + D] for at in (own, other) for x in stats]
            block = jnp.concatenate(parts + [jnp.zeros((STAT_ROWS - len(parts), D), f32)], axis=0).astype(bf16)
            for blk in range(D // STEP_LEN):
                k, at = k0 + g * (D // STEP_LEN) + blk, blk * STEP_LEN
                pay_ref[k, 0:STEP_LEN, :] = grad[own + at : own + at + STEP_LEN]
                pay_ref[k, STEP_LEN:CHUNK, :] = grad[other + at : other + at + STEP_LEN]
                pay_ref[k, CHUNK:, :] = block
        return total

    total = run(None)
    in_range = (jnp.min(total) > TOTAL_LOW) & (jnp.max(total) < TOTAL_HIGH)

    @pl.when(jnp.logical_not(in_range))
    def _():
        top = jnp.max(fold8(masked(dot_nt(keys, q_rows)), jnp.max), axis=0, keepdims=True)
        run((top * SCALE2).astype(bf16).astype(f32))


def key_grads(keys, values, q_rows, do_rows, out_dot, mask, log_total):
    scores = dot_nt(keys, q_rows)
    if mask is not None:
        scores = jnp.where(mask, scores, MASKED)
    probs = jnp.exp2(scores * SCALE2 - log_total)
    dscores = (probs * (dot_nt(values, do_rows) - out_dot)).astype(bf16)
    grad_k = (SCALE * dot_nn(dscores, q_rows)).astype(bf16)
    return grad_k, dot_nn(probs.astype(bf16), do_rows).astype(bf16)


def row_dots(own, other, head):
    parts = [x[pl.ds(GROUP * head + g, 1), :] for g in range(GROUP) for x in (own, other)]
    return jnp.concatenate(parts, axis=1)


def heads_of_step(kv, core, q, qx, do, dox, dots, dotsx):
    for i in range(PAIR):
        head = pl.program_id(0) * PAIR + i
        yield i, head, head_rows(q, qx, i), head_rows(do, dox, i), row_dots(dots, dotsx, core * kv + head)


def prompt_kernel(place, q, qx, do, dox, dots, dotsx, kp, vp, pay, stat):
    kv = stat.shape[1]
    for i, head, q_rows, do_rows, out_dot in heads_of_step(kv, place[1], q, qx, do, dox, dots, dotsx):
        at = slice(i * D, (i + 1) * D)
        attend(kp[:, at], vp[:, at], q_rows, do_rows, out_dot, None, pay, stat, head, i * (pay.shape[0] // PAIR))


def prompt_grads_kernel(place, log_total, q, qx, do, dox, dots, dotsx, kp, vp, grad_k, grad_v):
    kv = log_total.shape[0]
    for i, head, q_rows, do_rows, out_dot in heads_of_step(kv, place[1], q, qx, do, dox, dots, dotsx):
        at = slice(i * D, (i + 1) * D)
        grad_k[:, at], grad_v[:, at] = key_grads(
            kp[:, at], vp[:, at], q_rows, do_rows, out_dot, None, log_total[pl.ds(head, 1), :]
        )


def sibling_mask(parents, core, half):
    steps = 2 * half // STEP_LEN
    reached = []
    for s in range(steps):
        bits = jnp.int32(1 << s)
        for t in range(s):
            bits = bits | jnp.where(parents[s] == t, reached[t], 0)
        reached.append(bits)

    def token(index):
        other_core = jnp.bitwise_xor((index // half) % 2, core)
        return other_core * (steps // 2) + (index % half) // STEP_LEN, index % STEP_LEN

    row_step, row_at = token(lax.broadcasted_iota(jnp.int32, (1, 2 * GROUP * half), 1))
    key_step, key_at = token(lax.broadcasted_iota(jnp.int32, (2 * half, 1), 0))
    row_bits = jnp.zeros(row_step.shape, jnp.int32)
    for s in range(steps):
        row_bits = jnp.where(row_step == s, reached[s], row_bits)
    seen = jnp.bitwise_and(jnp.right_shift(row_bits, key_step), 1) > 0
    return seen & ((key_step != row_step) | (key_at <= row_at))


def sibling_kernel(place, parents, q, qx, do, dox, dots, dotsx, ks, ksx, vs, vsx, pay, stat):
    kv = stat.shape[1]
    mask = sibling_mask(parents, place[1], ks.shape[0])
    for i, head, q_rows, do_rows, out_dot in heads_of_step(kv, place[1], q, qx, do, dox, dots, dotsx):
        at = slice(i * D, (i + 1) * D)
        keys = jnp.concatenate([ks[:, at], ksx[:, at]], axis=0)
        values = jnp.concatenate([vs[:, at], vsx[:, at]], axis=0)
        attend(keys, values, q_rows, do_rows, out_dot, mask, pay, stat, head, i * (pay.shape[0] // PAIR))


def sibling_grads_kernel(place, parents, log_total, q, qx, do, dox, dots, dotsx, ks, ksx, vs, vsx, gk, gkx, gv, gvx):
    kv = log_total.shape[0]
    half = ks.shape[0]
    mask = sibling_mask(parents, place[1], half)
    for i, head, q_rows, do_rows, out_dot in heads_of_step(kv, place[1], q, qx, do, dox, dots, dotsx):
        at = slice(i * D, (i + 1) * D)
        keys = jnp.concatenate([ks[:, at], ksx[:, at]], axis=0)
        values = jnp.concatenate([vs[:, at], vsx[:, at]], axis=0)
        grad_k, grad_v = key_grads(keys, values, q_rows, do_rows, out_dot, mask, log_total[pl.ds(head, 1), :])
        gk[:, at], gkx[:, at] = grad_k[:half], grad_k[half:]
        gv[:, at], gvx[:, at] = grad_v[:half], grad_v[half:]


def merge_kernel(place, got, mine, out, weight, total_ref):
    seq, core = place[0], place[1]
    sources = got.shape[0]
    at = pl.ds(pl.multiple_of((seq % (D // STEP_LEN)) * STEP_LEN, STEP_LEN), STEP_LEN)
    stats = got[:, CHUNK:, :].astype(f32)
    sib = mine[0, CHUNK:, :].astype(f32)
    plain = jnp.max(jnp.abs(jnp.concatenate([stats[:, 0], stats[:, 3], sib[0:1], sib[3:4]], axis=0))) == 0.0
    for half in range(2):
        r = 3 * half
        reference, total = stats[:, r, :], stats[:, r + 1, :] + stats[:, r + 2, :]
        sib_reference, sib_total = sib[r : r + 1], sib[r + 1 : r + 2] + sib[r + 2 : r + 3]
        top = jnp.maximum(jnp.max(reference, axis=0, keepdims=True), sib_reference)
        row_total = jnp.sum(jnp.exp2(reference - top) * total, axis=0, keepdims=True) + jnp.exp2(sib_reference - top) * sib_total
        log_total = top + jnp.log2(row_total)
        weight[half] = jnp.concatenate(
            [
                SCALE * jnp.exp2(reference - log_total),
                SCALE * jnp.exp2(sib_reference - log_total),
                jnp.zeros((D - sources - 1, D), f32),
            ],
            axis=0,
        ).T

    @pl.when(plain)
    def _():
        acc = mine[0, 0:CHUNK, :].astype(f32)
        for i in range(sources):
            acc = acc + got[i, 0:CHUNK, :].astype(f32)
        total_ref[0] = acc[:STEP_LEN] * weight[0, at, :][:, 0:1]
        total_ref[1] = acc[STEP_LEN:] * weight[1, at, :][:, 0:1]

    @pl.when(jnp.logical_not(plain))
    def _():
        for half in range(2):
            weights = weight[half, at, :]
            rows = slice(half * STEP_LEN, (half + 1) * STEP_LEN)
            acc = weights[:, sources : sources + 1] * mine[0, rows, :].astype(f32)
            for i in range(sources):
                acc = acc + weights[:, i : i + 1] * got[i, rows, :].astype(f32)
            total_ref[half] = acc

    own, other = total_ref[0], total_ref[1]
    first = jnp.where(core == 0, own, other).astype(bf16)
    second = jnp.where(core == 0, other, own).astype(bf16)
    for i in range(sources):
        out[2 * i] = first
        out[2 * i + 1] = second


def assemble_kernel(got, grad_q):
    kv, group, blocks, cores = got.shape[:4]
    blk = pl.program_id(0)
    for c in range(cores):
        for n in range(kv):
            for g in range(group):
                at = ((c * kv + n) * group + g) * D
                grad_q[:, at : at + D] = got[n, g, blk, c]


def join_kernel(place, ks, ksx, vs, vsx, grad_ks, grad_vs):
    width = ks.shape[1]

    @pl.when(place[1] == 0)
    def _():
        grad_ks[:, :width], grad_ks[:, width:] = ks[...], ksx[...]
        grad_vs[:, :width], grad_vs[:, width:] = vs[...], vsx[...]

    @pl.when(place[1] != 0)
    def _():
        grad_ks[:, :width], grad_ks[:, width:] = ksx[...], ks[...]
        grad_vs[:, :width], grad_vs[:, width:] = vsx[...], vs[...]


def combine(parts):
    top = functools.reduce(jnp.maximum, [x[0] for x in parts])
    return jnp.stack([top, sum(x[1] * jnp.exp2(x[0] - top) for x in parts)])


def total_over_seq(stat, size):
    stride = 1
    while stride < size:

        def moved(i, d):
            at = (i // stride) % RADIX
            return i + ((at + d) % RADIX - at) * stride

        others = [lax.ppermute(stat, "seq", [(i, moved(i, d)) for i in range(size)]) for d in range(1, RADIX)]
        stat = combine([stat] + others)
        stride *= RADIX
    return stat


def in_hbm(*arrays):
    return [pltpu.with_memory_space_constraint(x, pltpu.HBM) for x in arrays]


def local(query, d_out, out_fwd, prompt_keys, prompt_value_rows, sibling_key_rows, sibling_value_rows, parents):
    seq, core = lax.axis_index("seq"), lax.axis_index("head")
    place = jnp.stack([seq, core]).astype(jnp.int32)
    devices = lax.axis_size("seq")
    kv = prompt_keys.shape[1] // D
    count = prompt_keys.shape[0]
    tokens = query.shape[0]
    rows = 2 * GROUP * tokens
    chunks = devices // kv
    blocks = tokens // STEP_LEN
    steps = kv // PAIR
    params = pltpu.CompilerParams(vmem_limit_bytes=VMEM_LIMIT, dimension_semantics=("arbitrary",))
    whole = pl.BlockSpec(memory_space=pltpu.VMEM)
    bf = lambda *shape: jax.ShapeDtypeStruct(shape, bf16)

    def swap(x):
        return lax.ppermute(x, "head", SWAP)

    def call(kernel, name, prefetch, grid, in_specs, out_specs, out_shape, args, flops=0, exps=0, scratch=()):
        return pl.pallas_call(
            kernel,
            grid_spec=pltpu.PrefetchScalarGridSpec(
                num_scalar_prefetch=len(prefetch),
                grid=(grid,),
                in_specs=in_specs,
                out_specs=out_specs,
                scratch_shapes=scratch,
            ),
            out_shape=out_shape,
            compiler_params=params,
            cost_estimate=pl.CostEstimate(flops=flops, bytes_accessed=1 << 22, transcendentals=exps),
            name=name,
        )(*prefetch, *args)

    step_q = pl.BlockSpec((tokens, PAIR * GROUP * D), lambda n, p, *_: (0, p[1] * steps + n))
    step_k = pl.BlockSpec((tokens, PAIR * D), lambda n, p, *_: (0, p[1] * steps + n))
    step_cols = lambda size: pl.BlockSpec((size, PAIR * D), lambda n, *_: (0, n))

    qx, dox = swap(query), swap(d_out)
    dot_spec = pl.BlockSpec((tokens, 8 * D), lambda n: (0, n))
    dots = call(
        out_dot_kernel,
        "out_dot",
        (),
        query.shape[1] // (8 * D),
        [dot_spec] * 2,
        pl.BlockSpec((8, tokens), lambda n: (n, 0)),
        jax.ShapeDtypeStruct((query.shape[1] // D, tokens), f32),
        in_hbm(d_out, out_fwd),
    )
    dotsx = swap(dots)
    ksx, vsx = swap(sibling_key_rows), swap(sibling_value_rows)

    row_args = in_hbm(query, qx, d_out, dox) + [dots, dotsx]
    row_specs = [step_q] * 4 + [whole] * 2
    prompt_args = row_args + in_hbm(prompt_keys, prompt_value_rows)
    prompt_specs = row_specs + [step_cols(count)] * 2
    sib_args = row_args + in_hbm(sibling_key_rows, ksx, sibling_value_rows, vsx)
    sib_specs = row_specs + [step_k] * 4
    attend_specs = [
        pl.BlockSpec((chunks * PAIR, CHUNK + STAT_ROWS, D), lambda n, *_: (n, 0, 0)),
        whole,
    ]
    attend_shape = [bf(devices, CHUNK + STAT_ROWS, D), jax.ShapeDtypeStruct((2, kv, rows), f32)]
    work = kv * rows * D

    pay, stat = call(
        prompt_kernel,
        "prompt",
        (place,),
        steps,
        prompt_specs,
        attend_specs,
        attend_shape,
        prompt_args,
        6 * count * work,
        count * kv * rows,
    )
    got = lax.all_to_all(pay, "seq", split_axis=0, concat_axis=0, tiled=True)
    sib_pay, sib_stat = call(
        sibling_kernel,
        "sibling",
        (place, parents),
        steps,
        sib_specs,
        attend_specs,
        attend_shape,
        sib_args,
        12 * tokens * work,
        2 * tokens * kv * rows,
    )
    stats = combine([total_over_seq(stat, devices), sib_stat])
    log_total = stats[0] + jnp.log2(stats[1])
    got, log_total = lax.optimization_barrier((got, log_total))

    merged = call(
        merge_kernel,
        "merge",
        (place,),
        1,
        [
            pl.BlockSpec((devices, CHUNK + STAT_ROWS, D), lambda n, p: (0, 0, 0)),
            pl.BlockSpec((1, CHUNK + STAT_ROWS, D), lambda n, p: (p[0], 0, 0)),
        ],
        pl.BlockSpec((2 * devices, STEP_LEN, D), lambda n, p: (0, 0, 0)),
        bf(2 * devices, STEP_LEN, D),
        in_hbm(got, sib_pay),
        scratch=[pltpu.VMEM((2, D, D), f32), pltpu.VMEM((2, STEP_LEN, D), f32)],
    )
    grad_q = lax.all_to_all(merged, ("seq", "head"), split_axis=0, concat_axis=0, tiled=True)

    gks, gks_other, gvs, gvs_other = call(
        sibling_grads_kernel,
        "sibling_grads",
        (place, parents),
        steps,
        [whole] + sib_specs,
        [step_cols(tokens)] * 4,
        [bf(tokens, kv * D)] * 4,
        [log_total] + sib_args,
        16 * tokens * work,
        2 * tokens * kv * rows,
    )
    gks_other, gvs_other = swap(gks_other), swap(gvs_other)
    grad_kp, grad_vp = call(
        prompt_grads_kernel,
        "prompt_grads",
        (place,),
        steps,
        [whole] + prompt_specs,
        [step_cols(count)] * 2,
        [bf(count, kv * D)] * 2,
        [log_total] + prompt_args,
        8 * count * work,
        count * kv * rows,
    )
    grad_ks, grad_vs = call(
        join_kernel,
        "join",
        (place,),
        1,
        [pl.BlockSpec((tokens, kv * D), lambda n, *_: (0, 0))] * 4,
        [pl.BlockSpec((tokens, 2 * kv * D), lambda n, *_: (0, 0))] * 2,
        [bf(tokens, 2 * kv * D)] * 2,
        [gks, gks_other, gvs, gvs_other],
    )
    grad_q = call(
        assemble_kernel,
        "assemble",
        (),
        blocks,
        [pl.BlockSpec((kv, GROUP, blocks, 2, STEP_LEN, D), lambda n: (0, 0, 0, 0, 0, 0))],
        pl.BlockSpec((STEP_LEN, query.shape[1]), lambda n: (n, 0)),
        bf(*query.shape),
        in_hbm(grad_q.reshape(kv, GROUP, blocks, 2, STEP_LEN, D)),
    )
    return grad_q, grad_kp, grad_vp, grad_ks, grad_vs


def solution(mesh):
    in_specs = (
        P("head", None),
        P("head", None),
        P("head", None),
        P("seq", "head"),
        P("seq", "head"),
        P("head", None),
        P("head", None),
        P(),
    )
    out_specs = (
        P("head", None),
        P("seq", "head"),
        P("seq", "head"),
        P("head", None),
        P("head", None),
    )
    return jax.shard_map(local, mesh=mesh, in_specs=in_specs, out_specs=out_specs, check_vma=False)
```

time: 138 us -> 116 us (0.84); the launches traced: 137 us -> 116 us
  local copies, waits for them, and re-layouts: 35 us -> 6.62 us
  Pallas kernels: 45.1 us -> 56.1 us
  waiting for transfers between devices: 20.7 us -> 16.2 us
  starting transfers between devices: 34.8 us -> 36.3 us
    unnamed x54 -> x20, local copies, waits for them, and re-layouts: 35 us -> 6.62 us
    pallas_call x7 -> x8, Pallas kernels: 45.1 us -> 56.1 us  [call(): pl.pallas_call(kernel, grid_spec=pltpu.PrefetchScalarGridSpec(num_scalar_...]
    all_to_all x1, waiting for transfers between devices: 3.2 us -> 0.01 us  [local(): got = lax.all_to_all(pay, 'seq', split_axis=0, concat_axis=0, tiled=True)]
    all_to_all x1, starting transfers between devices: 7.21 us -> 8.96 us  [local(): lax.all_to_all(merged, ('seq', 'head'), split_axis=0, concat_axis=0, tile...]
  transfers between devices with their start and end apart: 18 -> 18, of which waited for: 7 -> 5; matrix products, arithmetic and copies ran while one was open for 0% -> 0% of each run, Pallas kernels for 15% -> 28%
where the time goes in v2:
time: 116 us
  Pallas kernels  56.1 us (48%)
  starting transfers between devices  36.3 us (31%)
  waiting for transfers between devices  16.2 us (14%)
  local copies, waits for them, and re-layouts  6.62 us (6%)
    pallas_call x8, Pallas kernels, call(): pl.pallas_call(kernel, grid_spec=pltpu.PrefetchScalarGridSpec(num_scalar_...  56.1 us
    ppermute x9, waiting for transfers between devices, total_over_seq(): lax.ppermute(stat, 'seq', [(i, moved(i, d)) for i in range(size)])  15.4 us
    all_to_all x1, starting transfers between devices, local(): got = lax.all_to_all(pay, 'seq', split_axis=0, concat_axis=0, tiled=True)  11.4 us
    ppermute x9, starting transfers between devices, total_over_seq(): lax.ppermute(stat, 'seq', [(i, moved(i, d)) for i in range(size)])  10.9 us
    all_to_all x1, starting transfers between devices, local(): lax.all_to_all(merged, ('seq', 'head'), split_axis=0, concat_axis=0, tile...  8.96 us
    unnamed x20, local copies, waits for them, and re-layouts  6.62 us
    ppermute x7, starting transfers between devices, swap(): return lax.ppermute(x, 'head', SWAP)  5.11 us
  transfers between devices with their start and end apart: 18, of which 5 were waited for; matrix products, arithmetic and copies ran while one was open for 0% of the time, Pallas kernels for 28%

profile of v2, /device:TPU:1, one launch (start us, length us, event | category | flops | bytes accessed | tf_op | source)
XLA Modules:
  0.0 116.3 jit_solution(1233341782942599165)
XLA Ops:
  0.6 1.5 %collective-permute-start = (bf16[128,4096]{1,0:T(8,128)(2,1)}, bf16[128,4096]{1,0:T(8,128)(2,1)S(1)}, u32[]{:S(2)}, u32[]{:S(2)}) collective-permute-start(bf16[128,4096]{1,0:T(8,128)(2,1)} %q.7), channel_id=1, source_target_pairs={{0,1},{1,0},{2,3},{3,2},{4,5},{5,4},{6,7},{7,6},{8,9},{9,8},{10,11... | collective-permute-start | bytes 3145736 | tf_op jit(solution)/shard_map/ppermute | solution.py:292
  2.1 0.1 collective-permute-start.1
  2.2 3.3 %out_dot.1.dots = f32[32,128]{1,0:T(8,128)S(1)} custom-call(bf16[128,4096]{1,0:T(8,128)(2,1)} %do.9, bf16[128,4096]{1,0:T(8,128)(2,1)} %o.1), custom_call_target="tpu_custom_call" | custom-call | bytes 4194304 | tf_op jit(solution)/shard_map/out_dot/pallas_call | solution.py:295
  5.5 0.4 collective-permute-start.2
  5.9 0.1 pad_add_fusion.place
  6.0 0.8 collective-permute-done.2.dotsx
  6.8 0.0 collective-permute-done.qx
  6.8 0.0 copy-start.4
  6.8 0.0 collective-permute-done.1.dox
  6.8 1.0 copy-done.4
  7.7 0.0 copy-start.5
  7.7 1.0 copy-done.5
  8.7 16.8 %prompt.1 = (bf16[64,80,128]{2,1,0:T(8,128)(2,1)}, f32[2,8,512]{2,1,0:T(8,128)S(1)}) custom-call(s32[2]{0:T(128)S(1)} %pad_add_fusion.place, bf16[128,4096]{1,0:T(8,128)(2,1)} %q.7, bf16[128,4096]{1,0:T(8,128)(2,1)} %copy-done.4, bf16[128,4096]{1,0:T(8,128)(2,1)} %do.9, bf16[128,4096]{1,0:T(8,128)(2,1)} %copy-done.5, f32[32,128]{1,0:T(8,128)S(1)} %out_dot.1.dots, ...), custom_call_target="tpu_custom_call" | custom-call | flops 3221225472 | bytes 4194304 | tf_op jit(solution)/shard_map/prompt/pallas_call | solution.py:295
  25.5 0.0 copy-start.6
  25.5 0.0 copy-start.7
  25.5 0.0 copy-start.1
  25.5 11.4 %all-to-all-start = ((bf16[64,80,128]{2,1,0:T(8,128)(2,1)}), bf16[64,80,128]{2,1,0:T(8,128)(2,1)S(1)}, u32[]{:S(2)}, u32[]{:S(2)}) async-start(bf16[64,80,128]{2,1,0:T(8,128)(2,1)} %get-tuple-element.19), calls=%async_computation | async-start | bytes 2621440 | tf_op jit(solution)/shard_map/all_to_all | solution.py:354
  36.9 2.3 %collective-permute-start.5 = (f32[2,8,512]{2,1,0:T(8,128)S(1)}, f32[2,8,512]{2,1,0:T(8,128)S(1)}, u32[]{:S(2)}, u32[]{:S(2)}) collective-permute-start(f32[2,8,512]{2,1,0:T(8,128)S(1)} %get-tuple-element.20), channel_id=1, source_target_pairs={{0,6},{2,0},{4,2},{6,4},{8,14},{10,8},{12,10},{14,12},{16,22},{18,... | collective-permute-start | bytes 98312 | tf_op jit(solution)/shard_map/ppermute | solution.py:266
  39.2 0.6 collective-permute-start.4
  39.8 0.6 collective-permute-start.3
  40.3 0.0 copy-done.6
  40.3 1.7 %collective-permute-start.12 = (bf16[128,2048]{1,0:T(8,128)(2,1)S(1)}, bf16[128,2048]{1,0:T(8,128)(2,1)S(1)}, u32[]{:S(2)}, u32[]{:S(2)}) collective-permute-start(bf16[128,2048]{1,0:T(8,128)(2,1)S(1)} %copy-done.6), channel_id=1, source_target_pairs={{0,1},{1,0},{2,3},{3,2},{4,5},{5,4},{6,7},{7,6},{8,9},{9,8},{10,11... | collective-permute-start | bytes 1572872 | tf_op jit(solution)/shard_map/ppermute | solution.py:292
  42.1 0.0 copy-done.7
  42.1 0.1 collective-permute-start.13
  42.2 10.5 %collective-permute-done.5 = f32[2,8,512]{2,1,0:T(8,128)S(1)} collective-permute-done((f32[2,8,512]{2,1,0:T(8,128)S(1)}, f32[2,8,512]{2,1,0:T(8,128)S(1)}, u32[]{:S(2)}, u32[]{:S(2)}) %collective-permute-start.5) | collective-permute-done | bytes 32800 | tf_op jit(solution)/shard_map/ppermute | solution.py:266
  52.6 1.5 %collective-permute-done.4 = f32[2,8,512]{2,1,0:T(8,128)S(1)} collective-permute-done((f32[2,8,512]{2,1,0:T(8,128)S(1)}, f32[2,8,512]{2,1,0:T(8,128)S(1)}, u32[]{:S(2)}, u32[]{:S(2)}) %collective-permute-start.4) | collective-permute-done | bytes 32800 | tf_op jit(solution)/shard_map/ppermute | solution.py:266
  54.1 0.0 collective-permute-done.3
  54.2 2.5 %collective-permute-start.8 = (f32[2,8,512]{2,1,0:T(8,128)S(1)}, f32[2,8,512]{2,1,0:T(8,128)S(1)}, u32[]{:S(2)}, u32[]{:S(2)}) collective-permute-start(f32[2,8,512]{2,1,0:T(8,128)S(1)} %pad_maximum_fusion), channel_id=1, source_target_pairs={{0,24},{2,26},{4,28},{6,30},{8,0},{10,2},{12,4},{14,6},{16,8},{18,... | collective-permute-start | bytes 98312 | tf_op jit(solution)/shard_map/ppermute | solution.py:266
  56.7 0.6 collective-permute-start.7
  57.2 0.6 collective-permute-start.6
  57.8 0.0 collective-permute-done.8
  57.8 3.1 %collective-permute-done.7 = f32[2,8,512]{2,1,0:T(8,128)S(1)} collective-permute-done((f32[2,8,512]{2,1,0:T(8,128)S(1)}, f32[2,8,512]{2,1,0:T(8,128)S(1)}, u32[]{:S(2)}, u32[]{:S(2)}) %collective-permute-start.7) | collective-permute-done | bytes 32800 | tf_op jit(solution)/shard_map/ppermute | solution.py:266
  60.9 0.3 collective-permute-done.6
  61.3 2.8 %collective-permute-start.11 = (f32[2,8,512]{2,1,0:T(8,128)S(1)}, f32[2,8,512]{2,1,0:T(8,128)S(1)}, u32[]{:S(2)}, u32[]{:S(2)}) collective-permute-start(f32[2,8,512]{2,1,0:T(8,128)S(1)} %pad_maximum_fusion.1), channel_id=1, source_target_pairs={{0,96},{2,98},{4,100},{6,102},{8,104},{10,106},{12,108},{14,110},{... | collective-permute-start | bytes 98312 | tf_op jit(solution)/shard_map/ppermute | solution.py:266
  64.1 0.4 collective-permute-start.10
  64.4 0.7 collective-permute-start.9
  65.1 0.0 collective-permute-done.12.ksx
  65.1 0.0 copy-start.8
  65.1 0.0 collective-permute-done.13.vsx
  65.1 0.8 copy-done.8
  65.9 0.8 copy-done.9
  66.7 0.0 copy-done.1
  66.7 8.7 %sibling.1 = (bf16[64,80,128]{2,1,0:T(8,128)(2,1)S(1)}, f32[2,8,512]{2,1,0:T(8,128)S(1)}) custom-call(s32[2]{0:T(128)S(1)} %pad_add_fusion.place, s32[8]{0:T(128)S(1)} %copy-done.1, bf16[128,4096]{1,0:T(8,128)(2,1)} %q.7, bf16[128,4096]{1,0:T(8,128)(2,1)} %copy-done.4, bf16[128,4096]{1,0:T(8,128)(2,1)} %do.9, bf16[128,4096]{1,0:T(8,128)(2,1)} %copy-done.5, ...), custom_call_target="tpu_custom_call" | custom-call | flops 805306368 | bytes 4194304 | tf_op jit(solution)/shard_map/sibling/pallas_call | solution.py:295
  75.5 0.0 copy-start
  75.5 1.0 copy-done
  76.5 0.0 collective-permute-done.11
  76.5 0.0 collective-permute-done.10
  76.5 0.0 collective-permute-done.9
  76.5 0.1 fusion.6.log_total
  76.6 0.0 all-to-all-done.got
  76.6 0.0 copy-start.2
  76.6 1.0 copy-done.2
  77.7 4.0 %merge.1 = bf16[128,32,128]{2,1,0:T(8,128)(2,1)} custom-call(s32[2]{0:T(128)S(1)} %pad_add_fusion.place, bf16[64,80,128]{2,1,0:T(8,128)(2,1)} %copy-done.2, bf16[64,80,128]{2,1,0:T(8,128)(2,1)} %copy-done), custom_call_target="tpu_custom_call" | custom-call | bytes 4194304 | tf_op jit(solution)/shard_map/merge/pallas_call | solution.py:295
  81.7 9.0 %all-to-all-start.1 = ((bf16[128,32,128]{2,1,0:T(8,128)(2,1)}), bf16[128,32,128]{2,1,0:T(8,128)(2,1)S(1)}, u32[]{:S(2)}, u32[]{:S(2)}) async-start(bf16[128,32,128]{2,1,0:T(8,128)(2,1)} %merge.1), calls=%async_computation.1 | async-start | bytes 2097152 | tf_op jit(solution)/shard_map/all_to_all | solution.py:385
  90.7 6.3 %sibling_grads.1 = (bf16[128,1024]{1,0:T(8,128)(2,1)S(1)}, bf16[128,1024]{1,0:T(8,128)(2,1)S(1)}, bf16[128,1024]{1,0:T(8,128)(2,1)S(1)}, bf16[128,1024]{1,0:T(8,128)(2,1)S(1)}) custom-call(s32[2]{0:T(128)S(1)} %pad_add_fusion.place, s32[8]{0:T(128)S(1)} %copy-done.1, f32[8,512]{1,0:T(8,128)S(1)} %fusion.6.log_total, bf16[128,4096]{1,0:T(8,128)(2,1)} %q.7, ...), custom_call_target="tpu_custom_call" | custom-call | flops 1073741824 | bytes 4194304 | tf_op jit(solution)/shard_map/sibling_grads/pallas_call | solution.py:295
  97.0 1.2 collective-permute-start.14
  98.2 0.1 collective-permute-start.15
  98.3 12.6 %prompt_grads.1 = (bf16[1024,1024]{1,0:T(8,128)(2,1)}, bf16[1024,1024]{1,0:T(8,128)(2,1)}) custom-call(s32[2]{0:T(128)S(1)} %pad_add_fusion.place, f32[8,512]{1,0:T(8,128)S(1)} %fusion.6.log_total, bf16[128,4096]{1,0:T(8,128)(2,1)} %q.7, bf16[128,4096]{1,0:T(8,128)(2,1)} %copy-done.4, bf16[128,4096]{1,0:T(8,128)(2,1)} %do.9, bf16[128,4096]{1,0:T(8,128)(2,1)} %copy-done.5, ...), custom_call_target="tpu_custom_call" | custom-call | flops 4294967296 | bytes 4194304 | tf_op jit(solution)/shard_map/prompt_grads/pallas_call | solution.py:295
  110.9 0.0 collective-permute-done.14.ksx
  110.9 0.0 collective-permute-done.15.vsx
  110.9 1.6 %join.1 = (bf16[128,2048]{1,0:T(8,128)(2,1)}, bf16[128,2048]{1,0:T(8,128)(2,1)}) custom-call(s32[2]{0:T(128)S(1)} %pad_add_fusion.place, bf16[128,1024]{1,0:T(8,128)(2,1)S(1)} %get-tuple-element.27.ks, bf16[128,1024]{1,0:T(8,128)(2,1)S(1)} %collective-permute-done.14.ksx, bf16[128,1024]{1,0:T(8,128)(2,1)S(1)} %get-tuple-element.29.vs, ...), custom_call_target="tpu_custom_call" | custom-call | bytes 4194304 | tf_op jit(solution)/shard_map/join/pallas_call | solution.py:295
  112.5 0.0 all-to-all-done.1
  112.5 1.0 copy-done.3
  113.5 2.8 %assemble.1 = bf16[128,4096]{1,0:T(8,128)(2,1)} custom-call(bf16[8,2,4,2,32,128]{5,4,3,2,1,0:T(8,128)(2,1)} %bitcast.257), custom_call_target="tpu_custom_call" | custom-call | bytes 4194304 | tf_op jit(solution)/shard_map/assemble/pallas_call | solution.py:295
  (6 shorter events, 0.1 us)
Async XLA Ops:
  0.6 6.1 %collective-permute-start = (bf16[128,4096]{1,0:T(8,128)(2,1)}, bf16[128,4096]{1,0:T(8,128)(2,1)S(1)}, u32[]{:S(2)}, u32[]{:S(2)}) collective-permute-start(bf16[128,4096]{1,0:T(8,128)(2,1)} %q.7), channel_id=1, source_target_pairs={{0,1},{1,0},{2,3},{3,2},{4,5},{5,4},{6,7},{7,6},{8,9},{9,8},{10,11... | collective-permute-start | bytes 3145736 | tf_op jit(solution)/shard_map/ppermute | solution.py:292
  2.1 4.6 %collective-permute-start.1 = (bf16[128,4096]{1,0:T(8,128)(2,1)}, bf16[128,4096]{1,0:T(8,128)(2,1)S(1)}, u32[]{:S(2)}, u32[]{:S(2)}) collective-permute-start(bf16[128,4096]{1,0:T(8,128)(2,1)} %do.9), channel_id=1, source_target_pairs={{0,1},{1,0},{2,3},{3,2},{4,5},{5,4},{6,7},{7,6},{8,9},{9,8},{10,11... | collective-permute-start | bytes 3145736 | tf_op jit(solution)/shard_map/ppermute | solution.py:292
  5.5 1.3 %collective-permute-start.2 = (f32[32,128]{1,0:T(8,128)S(1)}, f32[32,128]{1,0:T(8,128)S(1)}, u32[]{:S(2)}, u32[]{:S(2)}) collective-permute-start(f32[32,128]{1,0:T(8,128)S(1)} %out_dot.1.dots), channel_id=1, source_target_pairs={{0,1},{1,0},{2,3},{3,2},{4,5},{5,4},{6,7},{7,6},{8,9},{9,8},{10,11... | collective-permute-start | bytes 49160 | tf_op jit(solution)/shard_map/ppermute | solution.py:292
  6.8 1.0 copy-start.4
  7.7 1.0 copy-start.5
  25.5 14.8 %copy-start.6 = (bf16[128,2048]{1,0:T(8,128)(2,1)S(1)}, bf16[128,2048]{1,0:T(8,128)(2,1)}, u32[]{:S(2)}) copy-start(bf16[128,2048]{1,0:T(8,128)(2,1)} %ks.3) | copy-start | bytes 1572868
  25.5 16.6 %copy-start.7 = (bf16[128,2048]{1,0:T(8,128)(2,1)S(1)}, bf16[128,2048]{1,0:T(8,128)(2,1)}, u32[]{:S(2)}) copy-start(bf16[128,2048]{1,0:T(8,128)(2,1)} %vs.3) | copy-start | bytes 1572868
  25.5 41.2 %copy-start.1 = (s32[8]{0:T(128)S(1)}, s32[8]{0:T(128)}, u32[]{:S(2)}) copy-start(s32[8]{0:T(128)} %parents.3) | copy-start | bytes 100
  25.5 51.1 %all-to-all-start = ((bf16[64,80,128]{2,1,0:T(8,128)(2,1)}), bf16[64,80,128]{2,1,0:T(8,128)(2,1)S(1)}, u32[]{:S(2)}, u32[]{:S(2)}) async-start(bf16[64,80,128]{2,1,0:T(8,128)(2,1)} %get-tuple-element.19), calls=%async_computation | async-start | bytes 2621440 | tf_op jit(solution)/shard_map/all_to_all | solution.py:354
  36.9 15.7 %collective-permute-start.5 = (f32[2,8,512]{2,1,0:T(8,128)S(1)}, f32[2,8,512]{2,1,0:T(8,128)S(1)}, u32[]{:S(2)}, u32[]{:S(2)}) collective-permute-start(f32[2,8,512]{2,1,0:T(8,128)S(1)} %get-tuple-element.20), channel_id=1, source_target_pairs={{0,6},{2,0},{4,2},{6,4},{8,14},{10,8},{12,10},{14,12},{16,22},{18,... | collective-permute-start | bytes 98312 | tf_op jit(solution)/shard_map/ppermute | solution.py:266
  39.2 15.0 %collective-permute-start.4 = (f32[2,8,512]{2,1,0:T(8,128)S(1)}, f32[2,8,512]{2,1,0:T(8,128)S(1)}, u32[]{:S(2)}, u32[]{:S(2)}) collective-permute-start(f32[2,8,512]{2,1,0:T(8,128)S(1)} %get-tuple-element.20), channel_id=1, source_target_pairs={{0,4},{2,6},{4,0},{6,2},{8,12},{10,14},{12,8},{14,10},{16,20},{18,... | collective-permute-start | bytes 98312 | tf_op jit(solution)/shard_map/ppermute | solution.py:266
  39.8 14.4 %collective-permute-start.3 = (f32[2,8,512]{2,1,0:T(8,128)S(1)}, f32[2,8,512]{2,1,0:T(8,128)S(1)}, u32[]{:S(2)}, u32[]{:S(2)}) collective-permute-start(f32[2,8,512]{2,1,0:T(8,128)S(1)} %get-tuple-element.20), channel_id=1, source_target_pairs={{0,2},{2,4},{4,6},{6,0},{8,10},{10,12},{12,14},{14,8},{16,18},{18,... | collective-permute-start | bytes 98312 | tf_op jit(solution)/shard_map/ppermute | solution.py:266
  40.3 24.8 %collective-permute-start.12 = (bf16[128,2048]{1,0:T(8,128)(2,1)S(1)}, bf16[128,2048]{1,0:T(8,128)(2,1)S(1)}, u32[]{:S(2)}, u32[]{:S(2)}) collective-permute-start(bf16[128,2048]{1,0:T(8,128)(2,1)S(1)} %copy-done.6), channel_id=1, source_target_pairs={{0,1},{1,0},{2,3},{3,2},{4,5},{5,4},{6,7},{7,6},{8,9},{9,8},{10,11... | collective-permute-start | bytes 1572872 | tf_op jit(solution)/shard_map/ppermute | solution.py:292
  42.1 23.0 %collective-permute-start.13 = (bf16[128,2048]{1,0:T(8,128)(2,1)S(1)}, bf16[128,2048]{1,0:T(8,128)(2,1)S(1)}, u32[]{:S(2)}, u32[]{:S(2)}) collective-permute-start(bf16[128,2048]{1,0:T(8,128)(2,1)S(1)} %copy-done.7), channel_id=1, source_target_pairs={{0,1},{1,0},{2,3},{3,2},{4,5},{5,4},{6,7},{7,6},{8,9},{9,8},{10,11... | collective-permute-start | bytes 1572872 | tf_op jit(solution)/shard_map/ppermute | solution.py:292
  54.2 3.6 %collective-permute-start.8 = (f32[2,8,512]{2,1,0:T(8,128)S(1)}, f32[2,8,512]{2,1,0:T(8,128)S(1)}, u32[]{:S(2)}, u32[]{:S(2)}) collective-permute-start(f32[2,8,512]{2,1,0:T(8,128)S(1)} %pad_maximum_fusion), channel_id=1, source_target_pairs={{0,24},{2,26},{4,28},{6,30},{8,0},{10,2},{12,4},{14,6},{16,8},{18,... | collective-permute-start | bytes 98312 | tf_op jit(solution)/shard_map/ppermute | solution.py:266
  56.7 4.3 %collective-permute-start.7 = (f32[2,8,512]{2,1,0:T(8,128)S(1)}, f32[2,8,512]{2,1,0:T(8,128)S(1)}, u32[]{:S(2)}, u32[]{:S(2)}) collective-permute-start(f32[2,8,512]{2,1,0:T(8,128)S(1)} %pad_maximum_fusion), channel_id=1, source_target_pairs={{0,16},{2,18},{4,20},{6,22},{8,24},{10,26},{12,28},{14,30},{16,0},... | collective-permute-start | bytes 98312 | tf_op jit(solution)/shard_map/ppermute | solution.py:266
  57.2 4.0 %collective-permute-start.6 = (f32[2,8,512]{2,1,0:T(8,128)S(1)}, f32[2,8,512]{2,1,0:T(8,128)S(1)}, u32[]{:S(2)}, u32[]{:S(2)}) collective-permute-start(f32[2,8,512]{2,1,0:T(8,128)S(1)} %pad_maximum_fusion), channel_id=1, source_target_pairs={{0,8},{2,10},{4,12},{6,14},{8,16},{10,18},{12,20},{14,22},{16,24},... | collective-permute-start | bytes 98312 | tf_op jit(solution)/shard_map/ppermute | solution.py:266
  61.3 15.2 %collective-permute-start.11 = (f32[2,8,512]{2,1,0:T(8,128)S(1)}, f32[2,8,512]{2,1,0:T(8,128)S(1)}, u32[]{:S(2)}, u32[]{:S(2)}) collective-permute-start(f32[2,8,512]{2,1,0:T(8,128)S(1)} %pad_maximum_fusion.1), channel_id=1, source_target_pairs={{0,96},{2,98},{4,100},{6,102},{8,104},{10,106},{12,108},{14,110},{... | collective-permute-start | bytes 98312 | tf_op jit(solution)/shard_map/ppermute | solution.py:266
  64.1 12.4 %collective-permute-start.10 = (f32[2,8,512]{2,1,0:T(8,128)S(1)}, f32[2,8,512]{2,1,0:T(8,128)S(1)}, u32[]{:S(2)}, u32[]{:S(2)}) collective-permute-start(f32[2,8,512]{2,1,0:T(8,128)S(1)} %pad_maximum_fusion.1), channel_id=1, source_target_pairs={{0,64},{2,66},{4,68},{6,70},{8,72},{10,74},{12,76},{14,78},{16,80}... | collective-permute-start | bytes 98312 | tf_op jit(solution)/shard_map/ppermute | solution.py:266
  64.4 12.1 %collective-permute-start.9 = (f32[2,8,512]{2,1,0:T(8,128)S(1)}, f32[2,8,512]{2,1,0:T(8,128)S(1)}, u32[]{:S(2)}, u32[]{:S(2)}) collective-permute-start(f32[2,8,512]{2,1,0:T(8,128)S(1)} %pad_maximum_fusion.1), channel_id=1, source_target_pairs={{0,32},{2,34},{4,36},{6,38},{8,40},{10,42},{12,44},{14,46},{16,48}... | collective-permute-start | bytes 98312 | tf_op jit(solution)/shard_map/ppermute | solution.py:266
  65.1 0.8 copy-start.8
  65.9 0.8 copy-start.9
  75.5 1.1 copy-start
  76.6 1.1 copy-start.2
  81.7 30.8 %all-to-all-start.1 = ((bf16[128,32,128]{2,1,0:T(8,128)(2,1)}), bf16[128,32,128]{2,1,0:T(8,128)(2,1)S(1)}, u32[]{:S(2)}, u32[]{:S(2)}) async-start(bf16[128,32,128]{2,1,0:T(8,128)(2,1)} %merge.1), calls=%async_computation.1 | async-start | bytes 2097152 | tf_op jit(solution)/shard_map/all_to_all | solution.py:385
  97.0 13.9 %collective-permute-start.14 = (bf16[128,1024]{1,0:T(8,128)(2,1)S(1)}, bf16[128,1024]{1,0:T(8,128)(2,1)S(1)}, u32[]{:S(2)}, u32[]{:S(2)}) collective-permute-start(bf16[128,1024]{1,0:T(8,128)(2,1)S(1)} %get-tuple-element.28), channel_id=1, source_target_pairs={{0,1},{1,0},{2,3},{3,2},{4,5},{5,4},{6,7},{7,6},{8,9},{9,8},{10,11... | collective-permute-start | bytes 786440 | tf_op jit(solution)/shard_map/ppermute | solution.py:292
  98.2 12.7 %collective-permute-start.15 = (bf16[128,1024]{1,0:T(8,128)(2,1)S(1)}, bf16[128,1024]{1,0:T(8,128)(2,1)S(1)}, u32[]{:S(2)}, u32[]{:S(2)}) collective-permute-start(bf16[128,1024]{1,0:T(8,128)(2,1)S(1)} %get-tuple-element.30), channel_id=1, source_target_pairs={{0,1},{1,0},{2,3},{3,2},{4,5},{5,4},{6,7},{7,6},{8,9},{9,8},{10,11... | collective-permute-start | bytes 786440 | tf_op jit(solution)/shard_map/ppermute | solution.py:292
  112.5 1.0 copy-start.3
